TPU v7x, 32 devices: a whole 2x2x4 slice. The times are simulated.
32 devices in a mesh: seq: 8 (over z, core), head: 4 (over y, x).
Axes of the slice: x: 2, y: 2, z: 4, core: 2. Of those that a mesh axis runs over, the one named last changes fastest.
Arguments:
- queries: bfloat16 [2048, 2048], P('seq', 'head'), may hold values from -6 to 6
- key_states: bfloat16 [2048, 256], P('seq', 'head'), may hold values from -6 to 6
- value_states: bfloat16 [2048, 256], P('seq', 'head'), may hold values from -6 to 6
- block_picks: int32 [4, 2, 2], replicated, may hold values from 1 to 3, as said below
- grad_output: bfloat16 [2048, 2048], P('seq', 'head'), may hold values from -6 to 6
Outputs:
- attn_output: bfloat16 [2048, 2048], P('seq', 'head')
- grad_queries: float32 [2048, 2048], P('seq', 'head')
- grad_keys: float32 [2048, 256], P('seq', 'head')
- grad_values: float32 [2048, 256], P('seq', 'head')
Inputs may be any that keep to these rules, and one draw needn't show every extreme that they name: `block_picks`: for query block b and KV head g the offsets differ from each other and lie in 1 to max(b, 2).
All inputs are finite; a program needn't handle non-finite values.
Results may differ from a plain program's by a relative error of at most 0.0095.
Values may be sent and summed in bfloat16 or wider, within the bound.
A program may use at most 64 MiB of HBM per device.

v0:
```python
import jax
import jax.numpy as jnp
from jax import lax
from jax.sharding import PartitionSpec as P

BLOCK = 512


NEGATIVE = -1e30


def partner_2(shard, axis, apart):
    return lax.ppermute(shard, axis, [(i, i ^ 1 << apart) for i in range(lax.axis_size(axis))])


def columns(block_data, which_half, count):
    return lax.dynamic_slice_in_dim(block_data, which_half * count, count, block_data.ndim - 1)


def ordered(own_part, other_part, pair_half):
    return jnp.where(
        pair_half == 0,
        jnp.concatenate([own_part, other_part], -1),
        jnp.concatenate([other_part, own_part], -1),
    )


def local(queries, key_states, value_states, block_picks, grad_output):
    row_count = queries.shape[0]
    half_dim = key_states.shape[1]
    head_dim = 2 * half_dim
    local_heads = queries.shape[1] // head_dim
    seq_count = lax.axis_size("seq")
    seq_index = lax.axis_index("seq")
    pair_half = lax.axis_index("head") % 2
    kv_group = lax.axis_index("head") // 2
    num_blocks = block_picks.shape[0]
    stripe_rows = BLOCK // seq_count
    query_rows = min(row_count, BLOCK)
    query_blocks = row_count // query_rows
    chosen = block_picks.shape[2] + 1
    key_count = chosen * BLOCK
    scaling = head_dim ** (-0.5)
    group_picks = lax.dynamic_index_in_dim(block_picks, kv_group, 1, keepdims=False)
    block_starts = (jnp.arange(seq_count, dtype=jnp.int32) * row_count // BLOCK)[
        :, None
    ] + jnp.arange(query_blocks, dtype=jnp.int32)[None, :]
    wanted = jnp.concatenate(
        [
            block_starts[..., None],
            block_starts[..., None] - jnp.take(group_picks, block_starts, axis=0),
        ],
        -1,
    )
    own_ids = lax.dynamic_index_in_dim(wanted, seq_index, 0, keepdims=False)
    usable = own_ids >= 0
    block_ids = jnp.maximum(wanted, 0).reshape(-1)
    local_kv = jnp.concatenate([key_states, value_states], 1)
    col_width = local_kv.shape[1]
    spread = local_kv.reshape(row_count // seq_count, seq_count, col_width)
    banded = lax.all_to_all(spread, "seq", split_axis=1, concat_axis=0, tiled=True).reshape(
        num_blocks, stripe_rows, col_width
    )
    outgoing = jnp.take(banded, block_ids, axis=0).reshape(
        seq_count, query_blocks * chosen, stripe_rows, col_width
    )
    arrived = lax.all_to_all(outgoing, "seq", split_axis=0, concat_axis=0, tiled=True)
    fetched = arrived.transpose(1, 2, 0, 3).reshape(query_blocks, key_count, col_width)
    partner = partner_2(fetched, "head", 0)
    key_tiles = ordered(fetched[..., :half_dim], partner[..., :half_dim], pair_half)
    value_tiles = ordered(fetched[..., half_dim:], partner[..., half_dim:], pair_half)
    q_blocks = queries.reshape(query_blocks, query_rows, local_heads, head_dim)
    g_blocks = grad_output.reshape(query_blocks, query_rows, local_heads, head_dim)
    slot_index = jnp.arange(key_count, dtype=jnp.int32) // BLOCK
    key_place = jnp.arange(key_count, dtype=jnp.int32) % BLOCK
    query_place = (
        (seq_index * row_count + jnp.arange(row_count, dtype=jnp.int32)) % BLOCK
    ).reshape(query_blocks, query_rows)
    allowed = usable[:, slot_index][:, None, :] & (
        (slot_index > 0)[None, None, :] | (key_place[None, None, :] <= query_place[:, :, None])
    )
    scores = (
        jnp.einsum("nrhd,nkd->nhrk", q_blocks, key_tiles, preferred_element_type=jnp.float32)
        * scaling
    )
    scores = jnp.where(allowed[:, None], scores, NEGATIVE)
    row_max = jnp.max(scores, axis=-1, keepdims=True)
    weights = jnp.exp(scores - row_max)
    probs = weights / jnp.sum(weights, axis=-1, keepdims=True)
    probs_low = probs.astype(jnp.bfloat16)
    attended = jnp.einsum(
        "nhrk,nkd->nrhd", probs_low, value_tiles, preferred_element_type=jnp.float32
    )
    attn_output = attended.astype(jnp.bfloat16).reshape(row_count, -1)
    row_delta = jnp.sum(g_blocks.astype(jnp.float32) * attended, axis=-1)
    grad_prob = jnp.einsum(
        "nrhd,nkd->nhrk", g_blocks, value_tiles, preferred_element_type=jnp.float32
    )
    dscore = (probs * (grad_prob - jnp.transpose(row_delta, (0, 2, 1))[..., None])).astype(
        jnp.bfloat16
    )
    grad_queries = (
        jnp.einsum("nhrk,nkd->nrhd", dscore, key_tiles, preferred_element_type=jnp.float32)
        * scaling
    ).reshape(row_count, -1)
    grad_k = (
        jnp.einsum("nhrk,nrhd->nkd", dscore, q_blocks, preferred_element_type=jnp.float32) * scaling
    )
    grad_v = jnp.einsum("nhrk,nrhd->nkd", probs_low, g_blocks, preferred_element_type=jnp.float32)
    sent_cols = jnp.concatenate(
        [columns(grad_k, 1 - pair_half, half_dim), columns(grad_v, 1 - pair_half, half_dim)], -1
    )
    received = partner_2(sent_cols.astype(jnp.bfloat16), "head", 0).astype(sent_cols.dtype)
    returned = (
        jnp.concatenate(
            [columns(grad_k, pair_half, half_dim), columns(grad_v, pair_half, half_dim)], -1
        )
        + received
    )
    ret_width = returned.shape[-1]
    going_out = returned.reshape(
        query_blocks * chosen, stripe_rows, seq_count, ret_width
    ).transpose(2, 0, 1, 3)
    landed = lax.all_to_all(going_out, "seq", split_axis=0, concat_axis=0, tiled=True)
    member = (block_ids[:, None] == jnp.arange(num_blocks, dtype=jnp.int32)[None, :]).astype(
        jnp.float32
    )
    summed = jnp.dot(
        member.T,
        landed.reshape(-1, stripe_rows * ret_width),
        precision=lax.Precision.HIGHEST,
        preferred_element_type=jnp.float32,
    )
    back_rows = summed.reshape(seq_count, row_count // seq_count, 1, ret_width)
    owned_rows = lax.all_to_all(back_rows, "seq", split_axis=0, concat_axis=2, tiled=True).reshape(
        row_count, ret_width
    )
    return (attn_output, grad_queries, owned_rows[:, :half_dim], owned_rows[:, half_dim:])


def solution(mesh):
    return jax.shard_map(
        local,
        mesh=mesh,
        in_specs=(P("seq", "head"), P("seq", "head"), P("seq", "head"), P(), P("seq", "head")),
        out_specs=(P("seq", "head"), P("seq", "head"), P("seq", "head"), P("seq", "head")),
        check_vma=False,
    )
```

profile of v0, /device:TPU:0, one launch (start us, length us, event | category | flops | bytes accessed | tf_op | source)
XLA Modules:
  0.0 118.6 jit_solution(5470903357277886315)
XLA Ops:
  0.6 0.9 copy.56
  1.5 0.9 copy.55
  2.5 0.6 copy.57
  3.1 6.3 %all-to-all-start = ((bf16[32,8,128]{2,0,1:T(8,128)(2,1)}), bf16[32,8,128]{2,0,1:T(8,128)(2,1)S(1)}, u32[]{:S(2)}, u32[]{:S(2)}) async-start(bf16[32,8,128]{2,0,1:T(8,128)(2,1)} %copy.57), calls=%async_computation | async-start | bytes 131072 | tf_op jit(solution)/shard_map/all_to_all | solution.py:61
  9.7 0.6 gather_fusion
  10.7 0.5 fusion.50
  11.3 4.1 %all-to-all-done = bf16[32,8,128]{2,0,1:T(8,128)(2,1)S(1)} async-done(((bf16[32,8,128]{2,0,1:T(8,128)(2,1)}), bf16[32,8,128]{2,0,1:T(8,128)(2,1)S(1)}, u32[]{:S(2)}, u32[]{:S(2)}) %all-to-all-start) | async-done | bytes 65568 | tf_op jit(solution)/shard_map/all_to_all | solution.py:61
  15.4 0.6 gather_fusion.1
  16.0 0.9 broadcast_select_fusion
  16.9 3.5 %all-to-all-start.1 = ((bf16[8,3,64,128]{3,2,1,0:T(8,128)(2,1)}), bf16[8,3,64,128]{3,2,1,0:T(8,128)(2,1)S(1)}, u32[]{:S(2)}, u32[]{:S(2)}) async-start(bf16[8,3,64,128]{3,2,1,0:T(8,128)(2,1)} %broadcast_select_fusion), calls=%async_computation.1 | async-start | bytes 786432 | tf_op jit(solution)/shard_map/all_to_all | solution.py:67
  20.3 2.0 %select_reduce_fusion = pred[1536]{0:T(1024)(128)(4,1)S(1)} fusion(pred[]{:T(512)} %bitcast.14, pred[]{:T(512)} %bitcast.16, pred[]{:T(512)} %bitcast.15), kind=kLoop, calls=%fused_computation.47 | loop fusion | flops 23040 | bytes 1539 | tf_op jit(solution)/shard_map/gather | solution.py:79
  22.3 1.1 copy.64
  23.4 1.1 copy.88
  24.5 1.2 copy.87
  25.7 1.4 %or_and_fusion = pred[256,1536]{0,1:T(8,128)(4,1)S(1)} fusion(s32[256]{0:T(256)S(1)} %and_select_fusion.1, s32[1536]{0:T(1024)S(1)} %fusion.30, pred[1536]{0:T(1024)(128)(4,1)S(1)} %select_reduce_fusion, pred[1536]{0:T(1024)(128)(4,1)S(1)} %fusion.36), kind=kLoop, calls=%fused_computation.19 | loop fusion | flops 1179648 | bytes 403456 | tf_op jit(solution)/shard_map/and | solution.py:79
  27.1 5.7 %all-to-all-done.1 = bf16[8,3,64,128]{3,2,1,0:T(8,128)(2,1)S(1)} async-done(((bf16[8,3,64,128]{3,2,1,0:T(8,128)(2,1)}), bf16[8,3,64,128]{3,2,1,0:T(8,128)(2,1)S(1)}, u32[]{:S(2)}, u32[]{:S(2)}) %all-to-all-start.1) | async-done | bytes 393248 | tf_op jit(solution)/shard_map/all_to_all | solution.py:67
  32.8 0.3 copy.59
  33.1 1.6 %collective-permute-start = (bf16[1,1536,128]{2,1,0:T(8,128)(2,1)S(1)}, bf16[1,1536,128]{2,1,0:T(8,128)(2,1)S(1)}, u32[]{:S(2)}, u32[]{:S(2)}) collective-permute-start(bf16[1,1536,128]{2,1,0:T(8,128)(2,1)S(1)} %bitcast.146), channel_id=1, source_target_pairs={{0,1},{1,0},{2,3},{3,2},{4,5},{5,4},{6,7},{7,6},{8,9},{9,8},{10,11... | collective-permute-start | bytes 1179656 | tf_op jit(solution)/shard_map/ppermute | solution.py:13
  34.6 0.2 slice_bitcast_fusion.1
  34.8 9.0 %collective-permute-done = bf16[1,1536,128]{2,1,0:T(8,128)(2,1)S(1)} collective-permute-done((bf16[1,1536,128]{2,1,0:T(8,128)(2,1)S(1)}, bf16[1,1536,128]{2,1,0:T(8,128)(2,1)S(1)}, u32[]{:S(2)}, u32[]{:S(2)}) %collective-permute-start) | collective-permute-done | bytes 393248 | tf_op jit(solution)/shard_map/ppermute | solution.py:13
  43.8 0.2 slice_bitcast_fusion
  44.0 0.7 copy-done.2
  44.7 1.5 %fusion.4 = (f32[4,256]{1,0:T(4,128)S(1)}, f32[1536,256,4]{1,0,2:T(8,128)S(1)}) fusion(pred[256,1536]{0,1:T(8,128)(4,1)S(1)} %or_and_fusion, bf16[256,4,128]{0,2,1:T(8,128)(2,1)S(1)} %bitcast.154, bf16[1536,64]{1,0:T(8,128)(2,1)S(1)} %get-tuple-element.20, bf16[1536,64]{1,0:T(8,128)(2,1)S(1)} %get-tuple-element.18, pred[]{:T(512)S(6)} %eq.14), kind=kOutput, calls=%fused_computation.9 | convolution fusion | flops 409140224 | bytes 7344129 | tf_op jit(solution)/shard_map/nrhd,nkd->nhrk/dot_general | solution.py:83
  46.2 1.4 %fusion.3 = f32[4,256]{1,0:T(4,128)S(1)} fusion(f32[1536,256,4]{1,0,2:T(8,128)S(1)} %get-tuple-element.30, f32[4,256]{1,0:T(4,128)S(1)} %get-tuple-element.29, pred[256,1536]{0,1:T(8,128)(4,1)S(1)} %or_and_fusion), kind=kLoop, calls=%fused_computation.8 | loop fusion | flops 6290432 | bytes 6692864 | tf_op jit(solution)/shard_map/reduce_sum | solution.py:89
  47.6 2.0 %fusion.11 = f32[1536,128]{0,1:T(8,128)S(1)} fusion(bf16[256,4,128]{0,2,1:T(8,128)(2,1)S(1)} %bitcast.158, f32[4,256]{1,0:T(4,128)S(1)} %fusion.3, f32[4,256]{1,0:T(4,128)S(1)} %get-tuple-element.29, f32[1536,256,4]{1,0,2:T(8,128)S(1)} %get-tuple-element.30, pred[256,1536]{0,1:T(8,128)(4,1)S(1)} %or_and_fusion), kind=kOutput, calls=%fused_computation.16 | convolution fusion | flops 410517504 | bytes 7741440 | tf_op jit(solution)/shard_map/nhrk,nrhd->nkd/dot_general | solution.py:109
  49.6 3.1 %multiply_reduce_fusion = (f32[256,4]{0,1:T(4,128)S(1)}, bf16[1,256,4,128]{1,3,2,0:T(8,128)(2,1)}) fusion(f32[1,256,4,128]{1,3,2,0:T(8,128)S(1)} %bitcast.156, f32[4,256]{1,0:T(4,128)S(1)} %fusion.3, f32[4,256]{1,0:T(4,128)S(1)} %get-tuple-element.29, f32[1536,256,4]{1,0,2:T(8,128)S(1)} %get-tuple-element.30, pred[256,1536]{0,1:T(8,128)(4,1)S(1)} %or_and_fusion, ...), kind=kOutput, calls=%fused_computation.26 | convolution fusion | flops 412679168 | bytes 7876609 | tf_op jit(solution)/shard_map/nhrk,nkd->nrhd/dot_general | solution.py:91
  52.7 3.6 %fusion.5 = bf16[4,256,1536]{1,2,0:T(8,128)(2,1)S(1)} fusion(bf16[256,4,128]{0,2,1:T(8,128)(2,1)S(1)} %bitcast.159, f32[4,256]{1,0:T(4,128)S(1)} %bitcast.161, f32[4,256]{1,0:T(4,128)S(1)} %fusion.3, f32[4,256]{1,0:T(4,128)S(1)} %get-tuple-element.29, f32[1536,256,4]{1,0,2:T(8,128)S(1)} %get-tuple-element.30, pred[256,1536]{0,1:T(8,128)(4,1)} %copy-done.3, ...), kind=kOutput, calls=%fused_computation.10 | convolution fusion | flops 415432704 | bytes 10498049 | tf_op jit(solution)/shard_map/nrhd,nkd->nhrk/dot_general | solution.py:96
  56.3 1.1 fusion.14
  57.5 0.9 copy-done.1
  58.4 0.8 pad_maximum_fusion
  59.2 1.5 %collective-permute-start.1 = (bf16[1,1536,128]{1,2,0:T(8,128)(2,1)}, bf16[1,1536,128]{1,2,0:T(8,128)(2,1)}, u32[]{:S(2)}, u32[]{:S(2)}) collective-permute-start(bf16[1,1536,128]{1,2,0:T(8,128)(2,1)} %pad_maximum_fusion), channel_id=1, source_target_pairs={{0,1},{1,0},{2,3},{3,2},{4,5},{5,4},{6,7},{7,6},{8,9},{9,8},{10,11... | collective-permute-start | bytes 1179656 | tf_op jit(solution)/shard_map/ppermute | solution.py:13
  60.7 1.2 dynamic-slice_bitcast_fusion
  61.9 7.4 %collective-permute-done.1 = bf16[1,1536,128]{1,2,0:T(8,128)(2,1)} collective-permute-done((bf16[1,1536,128]{1,2,0:T(8,128)(2,1)}, bf16[1,1536,128]{1,2,0:T(8,128)(2,1)}, u32[]{:S(2)}, u32[]{:S(2)}) %collective-permute-start.1) | collective-permute-done | bytes 393248 | tf_op jit(solution)/shard_map/ppermute | solution.py:13
  69.3 2.0 %maximum_add_fusion = f32[1,1536,128]{1,2,0:T(8,128)} fusion(f32[1,1536,64]{1,2,0:T(8,128)S(1)} %get-tuple-element.32, f32[1,1536,64]{1,2,0:T(8,128)S(1)} %get-tuple-element.33, bf16[1,1536,128]{1,2,0:T(8,128)(2,1)} %collective-permute-done.1), kind=kLoop, calls=%fused_computation.25 | loop fusion | flops 589824 | bytes 1966080 | tf_op jit(solution)/shard_map/add | solution.py:115
  71.3 2.3 %copy.71 = f32[1,1536,128]{2,1,0:T(8,128)} copy(f32[1,1536,128]{1,2,0:T(8,128)} %maximum_add_fusion) | data formatting | bytes 1572864 | tf_op jit(solution)/shard_map/add | solution.py:115
  73.6 2.2 %copy.72 = f32[8,3,64,128]{3,2,1,0:T(8,128)} copy(f32[8,3,64,128]{3,0,2,1:T(8,128)} %bitcast.149) | data formatting | bytes 1572864 | tf_op jit(solution)/shard_map/transpose | solution.py:123
  75.8 4.2 %all-to-all-start.2 = ((f32[8,3,64,128]{3,2,1,0:T(8,128)}), f32[8,3,64,128]{3,2,1,0:T(8,128)}, u32[]{:S(2)}, u32[]{:S(2)}) async-start(f32[8,3,64,128]{3,2,1,0:T(8,128)} %copy.72), calls=%async_computation.2 | async-start | bytes 1572864 | tf_op jit(solution)/shard_map/all_to_all | solution.py:124
  80.0 1.8 %copy.75 = bf16[256,512]{1,0:T(8,128)(2,1)} copy(bf16[256,512]{0,1:T(8,128)(2,1)} %bitcast.160) | data formatting | bytes 524288
  81.8 19.2 %all-to-all-done.2 = f32[8,3,64,128]{3,2,1,0:T(8,128)} async-done(((f32[8,3,64,128]{3,2,1,0:T(8,128)}), f32[8,3,64,128]{3,2,1,0:T(8,128)}, u32[]{:S(2)}, u32[]{:S(2)}) %all-to-all-start.2) | async-done | bytes 786464 | tf_op jit(solution)/shard_map/all_to_all | solution.py:124
  101.0 2.6 %fusion.18 = f32[4,8192]{1,0:T(4,128)} fusion(f32[3,8,64,128]{3,2,1,0:T(8,128)} %bitcast.66, s32[24]{0:T(128)S(1)} %reshape.599), kind=kOutput, calls=%fused_computation.22 | convolution fusion | flops 9437280 | bytes 917600 | tf_op jit(solution)/shard_map/dot_general | solution.py:128
  103.6 1.7 %reshape.586 = f32[8,32,1,128]{3,1,0,2:T(8,128)} reshape(f32[4,8192]{1,0:T(4,128)} %fusion.18) | data formatting | bytes 262144 | tf_op jit(solution)/shard_map/reshape | solution.py:134
  105.3 4.0 %all-to-all-start.3 = ((f32[8,32,1,128]{3,1,2,0:T(8,128)}), f32[8,32,1,128]{3,1,2,0:T(8,128)}, u32[]{:S(2)}, u32[]{:S(2)}) async-start(f32[8,32,1,128]{3,1,2,0:T(8,128)} %bitcast.157), calls=%async_computation.3 | async-start | bytes 262144 | tf_op jit(solution)/shard_map/all_to_all | solution.py:135
  109.3 3.0 %convolution_multiply_fusion = f32[128,4,256]{2,0,1:T(8,128)} fusion(bf16[4,256,1536]{1,2,0:T(8,128)(2,1)S(1)} %fusion.5, bf16[1536,64]{1,0:T(8,128)(2,1)} %copy-done.2, bf16[1536,64]{1,0:T(8,128)(2,1)S(1)} %get-tuple-element.18, pred[]{:T(512)S(6)} %eq.14), kind=kOutput, calls=%fused_computation.20 | convolution fusion | flops 404553728 | bytes 4063233 | tf_op jit(solution)/shard_map/nhrk,nkd->nrhd/dot_general | solution.py:103
  112.2 2.0 %copy.76 = f32[256,512]{1,0:T(8,128)} copy(f32[256,512]{0,1:T(8,128)} %bitcast.150) | data formatting | bytes 1048576
  114.3 1.8 %all-to-all-done.3 = f32[8,32,1,128]{3,1,2,0:T(8,128)} async-done(((f32[8,32,1,128]{3,1,2,0:T(8,128)}), f32[8,32,1,128]{3,1,2,0:T(8,128)}, u32[]{:S(2)}, u32[]{:S(2)}) %all-to-all-start.3) | async-done | bytes 131104 | tf_op jit(solution)/shard_map/all_to_all | solution.py:135
  116.1 1.0 copy.95
  117.1 0.7 copy.77
  117.9 0.7 copy.78
  (38 shorter events, 0.9 us)
Async XLA Ops:
  0.6 8.9 %copy-start = (s32[4,2,2]{0,2,1:T(2,128)S(1)}, s32[4,2,2]{0,2,1:T(2,128)}, u32[]{:S(2)}) copy-start(s32[4,2,2]{0,2,1:T(2,128)} %param.8) | copy-start | bytes 196
  3.1 12.2 %all-to-all-start = ((bf16[32,8,128]{2,0,1:T(8,128)(2,1)}), bf16[32,8,128]{2,0,1:T(8,128)(2,1)S(1)}, u32[]{:S(2)}, u32[]{:S(2)}) async-start(bf16[32,8,128]{2,0,1:T(8,128)(2,1)} %copy.57), calls=%async_computation | async-start | bytes 131072 | tf_op jit(solution)/shard_map/all_to_all | solution.py:61
  16.9 15.9 %all-to-all-start.1 = ((bf16[8,3,64,128]{3,2,1,0:T(8,128)(2,1)}), bf16[8,3,64,128]{3,2,1,0:T(8,128)(2,1)S(1)}, u32[]{:S(2)}, u32[]{:S(2)}) async-start(bf16[8,3,64,128]{3,2,1,0:T(8,128)(2,1)} %broadcast_select_fusion), calls=%async_computation.1 | async-start | bytes 786432 | tf_op jit(solution)/shard_map/all_to_all | solution.py:67
  24.5 23.1 %copy-start.7 = (bf16[256,512]{0,1:T(8,128)(2,1)}, bf16[256,512]{0,1:T(8,128)(2,1)S(1)}, u32[]{:S(2)}) copy-start(bf16[256,512]{0,1:T(8,128)(2,1)S(1)} %copy.88) | copy-start | bytes 786436
  25.7 20.5 %copy-start.4 = (bf16[256,512]{0,1:T(8,128)(2,1)}, bf16[256,512]{0,1:T(8,128)(2,1)S(1)}, u32[]{:S(2)}) copy-start(bf16[256,512]{0,1:T(8,128)(2,1)S(1)} %copy.87) | copy-start | bytes 786436
  27.1 22.5 %copy-start.3 = (pred[256,1536]{0,1:T(8,128)(4,1)}, pred[256,1536]{0,1:T(8,128)(4,1)S(1)}, u32[]{:S(2)}) copy-start(pred[256,1536]{0,1:T(8,128)(4,1)S(1)} %or_and_fusion) | copy-start | bytes 1179652
  33.1 10.7 %collective-permute-start = (bf16[1,1536,128]{2,1,0:T(8,128)(2,1)S(1)}, bf16[1,1536,128]{2,1,0:T(8,128)(2,1)S(1)}, u32[]{:S(2)}, u32[]{:S(2)}) collective-permute-start(bf16[1,1536,128]{2,1,0:T(8,128)(2,1)S(1)} %bitcast.146), channel_id=1, source_target_pairs={{0,1},{1,0},{2,3},{3,2},{4,5},{5,4},{6,7},{7,6},{8,9},{9,8},{10,11... | collective-permute-start | bytes 1179656 | tf_op jit(solution)/shard_map/ppermute | solution.py:13
  44.0 0.7 copy-start.2
  49.6 7.9 %copy-start.6 = (f32[1536,128]{0,1:T(8,128)}, f32[1536,128]{0,1:T(8,128)S(1)}, u32[]{:S(2)}) copy-start(f32[1536,128]{0,1:T(8,128)S(1)} %fusion.11) | copy-start | bytes 2359300
  49.6 3.1 %copy-start.8 = (bf16[256,512]{0,1:T(8,128)(2,1)S(1)}, bf16[256,512]{0,1:T(8,128)(2,1)}, u32[]{:S(2)}) copy-start(bf16[256,512]{0,1:T(8,128)(2,1)} %copy-done.7) | copy-start | bytes 786436
  52.7 3.6 %copy-start.5 = (bf16[256,512]{0,1:T(8,128)(2,1)S(1)}, bf16[256,512]{0,1:T(8,128)(2,1)}, u32[]{:S(2)}) copy-start(bf16[256,512]{0,1:T(8,128)(2,1)} %copy-done.4) | copy-start | bytes 786436
  57.5 0.9 copy-start.1
  59.2 10.1 %collective-permute-start.1 = (bf16[1,1536,128]{1,2,0:T(8,128)(2,1)}, bf16[1,1536,128]{1,2,0:T(8,128)(2,1)}, u32[]{:S(2)}, u32[]{:S(2)}) collective-permute-start(bf16[1,1536,128]{1,2,0:T(8,128)(2,1)} %pad_maximum_fusion), channel_id=1, source_target_pairs={{0,1},{1,0},{2,3},{3,2},{4,5},{5,4},{6,7},{7,6},{8,9},{9,8},{10,11... | collective-permute-start | bytes 1179656 | tf_op jit(solution)/shard_map/ppermute | solution.py:13
  75.8 25.2 %all-to-all-start.2 = ((f32[8,3,64,128]{3,2,1,0:T(8,128)}), f32[8,3,64,128]{3,2,1,0:T(8,128)}, u32[]{:S(2)}, u32[]{:S(2)}) async-start(f32[8,3,64,128]{3,2,1,0:T(8,128)} %copy.72), calls=%async_computation.2 | async-start | bytes 1572864 | tf_op jit(solution)/shard_map/all_to_all | solution.py:124
  105.3 10.8 %all-to-all-start.3 = ((f32[8,32,1,128]{3,1,2,0:T(8,128)}), f32[8,32,1,128]{3,1,2,0:T(8,128)}, u32[]{:S(2)}, u32[]{:S(2)}) async-start(f32[8,32,1,128]{3,1,2,0:T(8,128)} %bitcast.157), calls=%async_computation.3 | async-start | bytes 262144 | tf_op jit(solution)/shard_map/all_to_all | solution.py:135
where the time goes:
time: 120 us; the launch traced here: 119 us
  waiting for transfers between devices  47.1 us (39%)
  local copies, waits for them, and re-layouts  23.9 us (20%)
  starting transfers between devices  21 us (18%)
  matrix products  16.9 us (14%)
  other arithmetic  8.63 us (7%)
    all_to_all x1, waiting for transfers between devices, local(): lax.all_to_all(going_out, 'seq', split_axis=0, concat_axis=0, tiled=True)  19.2 us
    ppermute x2, waiting for transfers between devices, partner_2(): lax.ppermute(shard, axis, [(i, i ^ 1 << apart) for i in range(lax.axis_si...  16.4 us
    unnamed x24, local copies, waits for them, and re-layouts  8.71 us
    all_to_all x1, starting transfers between devices, local(): lax.all_to_all(spread, 'seq', split_axis=1, concat_axis=0, tiled=True)  6.33 us
    all_to_all x1, waiting for transfers between devices, local(): lax.all_to_all(outgoing, 'seq', split_axis=0, concat_axis=0, tiled=True)  5.66 us
    all_to_all x1, starting transfers between devices, local(): lax.all_to_all(going_out, 'seq', split_axis=0, concat_axis=0, tiled=True)  4.22 us
    all_to_all x1, waiting for transfers between devices, local(): lax.all_to_all(spread, 'seq', split_axis=1, concat_axis=0, tiled=True)  4.12 us
    all_to_all x1, starting transfers between devices, local(): lax.all_to_all(back_rows, 'seq', split_axis=0, concat_axis=2, tiled=True)  4 us
  transfers between devices with their start and end apart: 6, of which 6 were waited for; matrix products, arithmetic and copies ran while one was open for 14% of the time, Pallas kernels for 0%

commit v1 on v0

v1 whole, which is shorter than its diff:
```python
import functools

import jax
import jax.numpy as jnp
from jax import lax
from jax.experimental import pallas as pl
from jax.experimental.pallas import tpu as pltpu
from jax.sharding import PartitionSpec as P

BLOCK = 512
NEGATIVE = -1e30
LOG2E = 1.4426950408889634
MESH = pl.DeviceIdType.MESH
F32 = jnp.float32
BF16 = jnp.bfloat16


def dot(a, b, contract):
    return lax.dot_general(a, b, ((contract[:1], contract[1:]), ((), ())), preferred_element_type=F32)


def kernel(
    seq_size, chosen, picks, k_in, v_in, q_hbm, g_hbm, attn_hbm, dq_hbm, dk_out, dv_out,
    kv, q4, g4, ev, dpv, p_low, ds_low, k_t, v_t, top, total, prod, attn_buf, dq_buf,
    part, core_in, x_out, x_in, summed, z_out, z_in,
    in_sem, out_sem, zs, zr, xs, xr, cs, cr, cs2, cr2, xs2, xr2, zs2, zr2,
):
    rows, half = k_in.shape
    dim = 2 * half
    heads = q4.shape[0]
    num_blocks = kv.shape[0]
    seq = lax.axis_index("seq")
    head = lax.axis_index("head")
    b, c = seq // 2, seq % 2
    x, group = head % 2, head // 2
    oc, ox = 1 - c, 1 - x
    core_dev = (2 * b + oc, head)
    x_dev = (seq, 2 * group + ox)
    scaling = dim ** (-0.5)
    rate = scaling * LOG2E

    def remote(src, dst, send, recv, dev):
        return pltpu.make_async_remote_copy(
            src_ref=src, dst_ref=dst, send_sem=send, recv_sem=recv, device_id=dev, device_id_type=MESH
        )

    loads = []
    for h in range(heads):
        cols = pl.ds(h * dim, dim)
        loads.append(pltpu.make_async_copy(q_hbm.at[:, cols], q4.at[h], in_sem.at[0, h]))
        loads.append(pltpu.make_async_copy(g_hbm.at[:, cols], g4.at[h], in_sem.at[1, h]))
    for load in loads:
        load.start()

    barrier = pltpu.get_barrier_semaphore()
    pl.semaphore_signal(barrier, inc=1, device_id=core_dev, device_id_type=MESH)
    pl.semaphore_signal(barrier, inc=1, device_id=x_dev, device_id_type=MESH)
    for d in range(1, num_blocks):
        other = lax.rem(b + d, num_blocks)
        pl.semaphore_signal(barrier, inc=1, device_id=(2 * other + c, head), device_id_type=MESH)
    kv[b, c, x] = jnp.concatenate([k_in[...], v_in[...]], axis=1)
    pl.semaphore_wait(barrier, num_blocks + 1)

    def z_gather(d):
        mine = kv.at[b, c, x]
        return remote(mine, mine, zs.at[d], zr.at[d], (2 * (b + d) + c, head))

    def z_arrival(d):
        piece = kv.at[b - d, c, x]
        return remote(piece, piece, zs.at[d], zr.at[d], (2 * (b - d) + c, head))

    def x_gather(d, side):
        piece = kv.at[b - d, c, side]
        return remote(piece, piece, xs.at[d], xr.at[d], x_dev)

    def core_gather(d, which, row_half):
        piece = kv.at[b - d, row_half, x if which == 0 else ox]
        return remote(piece, piece, cs.at[d, which], cr.at[d, which], core_dev)

    x_gather(0, x).start()
    for d in reversed(range(1, num_blocks)):
        @pl.when(b + d < num_blocks)
        def _():
            z_gather(d).start()
    core_gather(0, 0, c).start()

    def forward_z(d):
        @pl.when(d <= b)
        def _():
            z_arrival(d).wait_recv()
            x_gather(d, x).start()
            core_gather(d, 0, c).start()

    def forward_x(d):
        @pl.when(d <= b)
        def _():
            x_gather(d, ox).wait_recv()
            core_gather(d, 1, c).start()

    def settle(d):
        @pl.when(d <= b)
        def _():
            core_gather(d, 0, oc).wait_recv()
            core_gather(d, 1, oc).wait_recv()

    lane = lax.broadcasted_iota(jnp.int32, (BLOCK, dim), 1)
    low_lanes = lane < half

    def tiles(block):
        left = jnp.concatenate([kv[block, 0, 0], kv[block, 1, 0]], axis=0).astype(F32)
        right = jnp.concatenate([kv[block, 0, 1], kv[block, 1, 1]], axis=0).astype(F32)
        keys = jnp.where(low_lanes, left, pltpu.roll(right, half, 1))
        values = jnp.where(low_lanes, pltpu.roll(left, half, 1), right)
        return keys, values

    def first_pass(slot, keys, values, usable):
        key_low, value_low = keys.astype(BF16), values.astype(BF16)
        for h in range(heads):
            s = dot(key_low, q4[h], (1, 1))
            if slot == 0:
                place = lax.broadcasted_iota(jnp.int32, (BLOCK, rows), 0)
                query = lax.broadcasted_iota(jnp.int32, (BLOCK, rows), 1) + c * rows
                s = jnp.where(place <= query, s, NEGATIVE)
            m = jnp.max(s, axis=0, keepdims=True)
            e = jnp.exp2((s - m) * rate)
            dp = dot(value_low, g4[h], (1, 1))
            ev[slot, h] = e
            dpv[slot, h] = dp
            top[slot, h] = m if slot == 0 else jnp.where(usable, m, NEGATIVE)
            total[slot, h] = jnp.sum(e, axis=0, keepdims=True)
            prod[slot, h] = jnp.sum(e * dp, axis=0, keepdims=True)
        at = pl.ds(slot * BLOCK, BLOCK)
        k_t[:, at] = keys.T.astype(BF16)
        v_t[:, at] = values.T.astype(BF16)

    forward_x(0)
    if num_blocks > 1:
        forward_z(1)
    for load in loads:
        load.wait()
    settle(0)
    first_pass(0, *tiles(b), None)
    for d in range(2, num_blocks):
        forward_z(d)
        forward_x(d - 1)
    if num_blocks > 1:
        forward_x(num_blocks - 1)
    for d in range(1, num_blocks):
        settle(d)

    offsets = [None] + [picks[b, group, j] for j in range(chosen - 1)]
    for slot in range(1, chosen):
        wanted = b - offsets[slot]
        first_pass(slot, *tiles(jnp.maximum(wanted, 0)), wanted >= 0)

    shares, deltas = [], []
    for h in range(heads):
        m = top[0, h]
        for slot in range(1, chosen):
            m = jnp.maximum(m, top[slot, h])
        weight = [jnp.exp2((top[slot, h] - m) * rate) for slot in range(chosen)]
        norm = sum(weight[slot] * total[slot, h] for slot in range(chosen))
        share = [w / norm for w in weight]
        shares.append(share)
        deltas.append(sum(share[slot] * prod[slot, h] for slot in range(chosen)))

    def core_return(slot):
        return remote(part.at[slot, oc], core_in.at[slot], cs2.at[slot], cr2.at[slot], core_dev)

    def x_return(slot):
        return remote(x_out.at[slot], x_in.at[slot], xs2.at[slot], xr2.at[slot], x_dev)

    def second_pass(slot):
        at = pl.ds(slot * BLOCK, BLOCK)
        grad_k = grad_v = None
        for h in range(heads):
            probs = ev[slot, h] * shares[h][slot]
            low = probs.astype(BF16)
            ds = (probs * (dpv[slot, h] - deltas[h])).astype(BF16)
            p_low[h, at] = low
            ds_low[h, at] = ds
            more_v = dot(low, g4[h], (1, 0))
            more_k = dot(ds, q4[h], (1, 0))
            grad_v = more_v if grad_v is None else grad_v + more_v
            grad_k = more_k if grad_k is None else grad_k + more_k
        grad_k = grad_k * scaling
        left = jnp.where(low_lanes, grad_k, pltpu.roll(grad_v, half, 1)).astype(BF16)
        right = jnp.where(low_lanes, pltpu.roll(grad_k, half, 1), grad_v).astype(BF16)
        for side in range(2):
            cut = slice(side * rows, (side + 1) * rows)
            part[slot, side, 0] = left[cut]
            part[slot, side, 1] = right[cut]
        core_return(slot).start()

    def cross(slot):
        core_return(slot).wait_recv()
        x_out[slot] = (part[slot, c, ox].astype(F32) + core_in[slot, ox].astype(F32)).astype(BF16)
        x_return(slot).start()
        summed[slot] = part[slot, c, x].astype(F32) + core_in[slot, x].astype(F32)

    def land(slot):
        x_return(slot).wait_recv()
        summed[slot] = summed[slot] + x_in[slot].astype(F32)

    def z_return(d):
        return remote(z_out.at[d], z_in.at[d], zs2.at[d], zr2.at[d], (2 * (b - d) + c, head))

    second_pass(1)
    for slot in range(2, chosen):
        second_pass(slot)
        cross(slot - 1)
    second_pass(0)
    cross(chosen - 1)
    cross(0)
    for slot in range(1, chosen):
        land(slot)
    for d in reversed(range(1, num_blocks)):
        @pl.when(d <= b)
        def _():
            z_out[d] = sum(
                jnp.where(offsets[slot] == d, summed[slot], 0.0) for slot in range(1, chosen)
            ).astype(BF16)
            z_return(d).start()

    stores = []
    for h in range(heads):
        attn_buf[h] = dot(v_t[...], p_low[h], (1, 0)).T.astype(BF16)
        dq_buf[h] = dot(k_t[...], ds_low[h], (1, 0)).T * scaling
        cols = pl.ds(h * dim, dim)
        stores.append(pltpu.make_async_copy(attn_buf.at[h], attn_hbm.at[:, cols], out_sem.at[0, h]))
        stores.append(pltpu.make_async_copy(dq_buf.at[h], dq_hbm.at[:, cols], out_sem.at[1, h]))
        stores[-2].start()
        stores[-1].start()

    land(0)
    for d in range(1, num_blocks):
        @pl.when(b + d < num_blocks)
        def _():
            z_return(d).wait_recv()
            summed[0] = summed[0] + z_in[d].astype(F32)
    owned = summed[0]
    dk_out[...] = owned[:, :half]
    dv_out[...] = owned[:, half:]

    for store in stores:
        store.wait()
    for d in range(num_blocks):
        @pl.when(d <= b)
        def _():
            x_gather(d, x).wait_send()
            core_gather(d, 0, c).wait_send()
            core_gather(d, 1, c).wait_send()
    for d in range(1, num_blocks):
        @pl.when(b + d < num_blocks)
        def _():
            z_gather(d).wait_send()
        @pl.when(d <= b)
        def _():
            z_return(d).wait_send()
    for slot in range(chosen):
        core_return(slot).wait_send()
        x_return(slot).wait_send()


def local(queries, key_states, value_states, block_picks, grad_output):
    rows, half = key_states.shape
    dim = 2 * half
    heads = queries.shape[1] // dim
    seq_size = lax.axis_size("seq")
    num_blocks = seq_size * rows // BLOCK
    assert BLOCK == 2 * rows
    chosen = block_picks.shape[2] + 1
    keys = chosen * BLOCK
    vmem = pl.BlockSpec(memory_space=pltpu.VMEM)
    anywhere = pl.BlockSpec(memory_space=pl.ANY)
    dma = pltpu.SemaphoreType.DMA
    return pl.pallas_call(
        functools.partial(kernel, seq_size, chosen),
        out_shape=(
            jax.ShapeDtypeStruct(queries.shape, BF16),
            jax.ShapeDtypeStruct(queries.shape, F32),
            jax.ShapeDtypeStruct(key_states.shape, F32),
            jax.ShapeDtypeStruct(value_states.shape, F32),
        ),
        in_specs=[pl.BlockSpec(memory_space=pltpu.SMEM), vmem, vmem, anywhere, anywhere],
        out_specs=(anywhere, anywhere, vmem, vmem),
        scratch_shapes=[
            pltpu.VMEM((num_blocks, 2, 2, rows, dim), BF16),
            pltpu.VMEM((heads, rows, dim), BF16),
            pltpu.VMEM((heads, rows, dim), BF16),
            pltpu.VMEM((chosen, heads, BLOCK, rows), F32),
            pltpu.VMEM((chosen, heads, BLOCK, rows), F32),
            pltpu.VMEM((heads, keys, rows), BF16),
            pltpu.VMEM((heads, keys, rows), BF16),
            pltpu.VMEM((dim, keys), BF16),
            pltpu.VMEM((dim, keys), BF16),
            pltpu.VMEM((chosen, heads, 1, rows), F32),
            pltpu.VMEM((chosen, heads, 1, rows), F32),
            pltpu.VMEM((chosen, heads, 1, rows), F32),
            pltpu.VMEM((heads, rows, dim), BF16),
            pltpu.VMEM((heads, rows, dim), F32),
            pltpu.VMEM((chosen, 2, 2, rows, dim), BF16),
            pltpu.VMEM((chosen, 2, rows, dim), BF16),
            pltpu.VMEM((chosen, rows, dim), BF16),
            pltpu.VMEM((chosen, rows, dim), BF16),
            pltpu.VMEM((chosen, rows, dim), F32),
            pltpu.VMEM((num_blocks, rows, dim), BF16),
            pltpu.VMEM((num_blocks, rows, dim), BF16),
            dma((2, heads)),
            dma((2, heads)),
            dma((num_blocks,)),
            dma((num_blocks,)),
            dma((num_blocks,)),
            dma((num_blocks,)),
            dma((num_blocks, 2)),
            dma((num_blocks, 2)),
            dma((chosen,)),
            dma((chosen,)),
            dma((chosen,)),
            dma((chosen,)),
            dma((num_blocks,)),
            dma((num_blocks,)),
        ],
        compiler_params=pltpu.CompilerParams(
            collective_id=0, has_side_effects=True, vmem_limit_bytes=56 * 1024 * 1024
        ),
        cost_estimate=pl.CostEstimate(
            flops=10 * heads * rows * keys * dim, bytes_accessed=4 * queries.size * 4, transcendentals=heads * rows * keys
        ),
    )(block_picks, key_states, value_states, queries, grad_output)


def solution(mesh):
    return jax.shard_map(
        local,
        mesh=mesh,
        in_specs=(P("seq", "head"), P("seq", "head"), P("seq", "head"), P(), P("seq", "head")),
        out_specs=(P("seq", "head"), P("seq", "head"), P("seq", "head"), P("seq", "head")),
        check_vma=False,
    )
```

time: 120 us -> 44.9 us (0.37)
  waiting for transfers between devices: 47.1 us -> 0 us
  Pallas kernels: 0 us -> 34.6 us
  starting transfers between devices: 21 us -> 0 us
  matrix products: 16.9 us -> 0 us
  local copies, waits for them, and re-layouts: 23.9 us -> 9.35 us
  other arithmetic: 8.63 us -> 0 us
    pallas_call x0 -> x1, Pallas kernels: none -> 34.6 us  [local(): pl.pallas_call(functools.partial(kernel, seq_size, chosen), out_shape=(ja...]
    all_to_all x4 -> x0, waiting for transfers between devices: 30.7 us -> none  [the longest x1 19.2 us: local(): lax.all_to_all(going_out, 'seq', split_axis=0, concat_axis=0, tiled=True)]
    all_to_all x4 -> x0, starting transfers between devices: 18 us -> none  [the longest x1 6.33 us: local(): lax.all_to_all(spread, 'seq', split_axis=1, concat_axis=0, tiled=True)]
    dot_general x7 -> x0, matrix products: 16.9 us -> none  [the longest x1 3.58 us: local(): jnp.einsum('nrhd,nkd->nhrk', g_blocks, value_tiles, preferred_element_typ...]
    ppermute x2 -> x0, waiting for transfers between devices: 16.4 us -> none  [partner_2(): lax.ppermute(shard, axis, [(i, i ^ 1 << apart) for i in range(lax.axis_si...]
    pallas_call x0 -> x2, local copies, waits for them, and re-layouts: none -> 3.29 us  [local(): pl.pallas_call(functools.partial(kernel, seq_size, chosen), out_shape=(ja...]
    ppermute x2 -> x0, starting transfers between devices: 3.05 us -> none  [partner_2(): lax.ppermute(shard, axis, [(i, i ^ 1 << apart) for i in range(lax.axis_si...]
    unnamed x24 -> x9, local copies, waits for them, and re-layouts: 8.71 us -> 6.06 us
  transfers between devices with their start and end apart: 6 -> 0, of which waited for: 6 -> 0; matrix products, arithmetic and copies ran while one was open for 14% -> 0% of each run, Pallas kernels for 0% -> 0%
where the time goes in v1:
time: 44.9 us; the launch traced here: 44.6 us
  Pallas kernels  34.6 us (77%)
  local copies, waits for them, and re-layouts  9.35 us (21%)
  between operations  0.65 us (1%)
    pallas_call x1, Pallas kernels, local(): pl.pallas_call(functools.partial(kernel, seq_size, chosen), out_shape=(ja...  34.6 us
    unnamed x9, local copies, waits for them, and re-layouts  6.06 us
    pallas_call x2, local copies, waits for them, and re-layouts, local(): pl.pallas_call(functools.partial(kernel, seq_size, chosen), out_shape=(ja...  3.29 us

profile of v1, /device:TPU:0, one launch (start us, length us, event | category | flops | bytes accessed | tf_op | source)
XLA Modules:
  0.0 44.6 jit_solution(10809161023092505044)
XLA Ops:
  0.6 1.4 %copy.9.picks = s32[4,2,2]{2,1,0:T(2,128)} copy(s32[4,2,2]{0,2,1:T(2,128)} %param.8) | data formatting | bytes 128 | tf_op args[3]
  2.0 0.0 copy-start.1
  2.0 1.5 %copy.10.k_in = bf16[256,64]{1,0:T(8,128)(2,1)} copy(bf16[256,64]{0,1:T(8,128)(2,1)} %param.6) | data formatting | bytes 65536 | tf_op args[1]
  3.5 0.0 copy-done.1
  3.5 0.7 %copy.11.v_in = bf16[256,64]{1,0:T(8,128)(2,1)} copy(bf16[256,64]{0,1:T(8,128)(2,1)S(1)} %copy-done.1) | data formatting | bytes 65536 | tf_op args[2]
  4.2 34.6 %shard_map.84 = (bf16[256,512]{1,0:T(8,128)(2,1)}, f32[256,512]{1,0:T(8,128)}, f32[256,64]{1,0:T(8,128)}, f32[256,64]{1,0:T(8,128)}) custom-call(s32[4,2,2]{2,1,0:T(2,128)} %copy.9.picks, bf16[256,64]{1,0:T(8,128)(2,1)} %copy.10.k_in, bf16[256,64]{1,0:T(8,128)(2,1)} %copy.11.v_in, bf16[256,512]{1,0:T(8,128)(2,1)} %q_hbm.1, bf16[256,512]{1,0:T(8,128)(2,1)} %g_hbm.1), custom_call_target="tpu_custom_call" | custom-call | flops 2013265920 | bytes 2097152 | tf_op jit(solution)/shard_map/pallas_call | solution.py:277
  38.8 0.0 copy-start
  38.8 1.7 %copy.12 = f32[256,64]{0,1:T(8,128)} copy(f32[256,64]{1,0:T(8,128)} %get-tuple-element.6) | data formatting | bytes 131072 | tf_op jit(solution)/shard_map/pallas_call | solution.py:277
  40.5 1.6 %copy.13 = f32[256,64]{0,1:T(8,128)} copy(f32[256,64]{1,0:T(8,128)} %get-tuple-element.7) | data formatting | bytes 131072 | tf_op jit(solution)/shard_map/pallas_call | solution.py:277
  42.1 1.7 %copy.16 = bf16[256,512]{1,0:T(8,128)(2,1)} copy(bf16[256,512]{1,0:T(8,128)(2,1)} %get-tuple-element.12) | data formatting | bytes 524288
  43.8 0.0 copy-done
  43.8 0.8 %copy.17 = f32[256,512]{1,0:T(8,128)} copy(f32[256,512]{1,0:T(8,128)S(1)} %copy-done) | data formatting | bytes 1048576
Async XLA Ops:
  2.0 1.5 %copy-start.1 = (bf16[256,64]{0,1:T(8,128)(2,1)S(1)}, bf16[256,64]{0,1:T(8,128)(2,1)}, u32[]{:S(2)}) copy-start(bf16[256,64]{0,1:T(8,128)(2,1)} %param.7) | copy-start | bytes 98308
  38.8 5.0 %copy-start = (f32[256,512]{1,0:T(8,128)S(1)}, f32[256,512]{1,0:T(8,128)}, u32[]{:S(2)}) copy-start(f32[256,512]{1,0:T(8,128)} %get-tuple-element.13) | copy-start | bytes 1572868

commit v2 on v1

--- a/solution.py
+++ b/solution.py
@@ -20,12 +20,12 @@
 
 
 def kernel(
-    seq_size, chosen, picks, k_in, v_in, q_hbm, g_hbm, attn_hbm, dq_hbm, dk_out, dv_out,
+    seq_size, chosen, picks, k_in, v_in, q_hbm, g_hbm, attn_hbm, dq_hbm, grads_out,
     kv, q4, g4, ev, dpv, p_low, ds_low, k_t, v_t, top, total, prod, attn_buf, dq_buf,
     part, core_in, x_out, x_in, summed, z_out, z_in,
     in_sem, out_sem, zs, zr, xs, xr, cs, cr, cs2, cr2, xs2, xr2, zs2, zr2,
 ):
-    rows, half = k_in.shape
+    half, rows = k_in.shape
     dim = 2 * half
     heads = q4.shape[0]
     num_blocks = kv.shape[0]
@@ -58,16 +58,17 @@
     for d in range(1, num_blocks):
         other = lax.rem(b + d, num_blocks)
         pl.semaphore_signal(barrier, inc=1, device_id=(2 * other + c, head), device_id_type=MESH)
-    kv[b, c, x] = jnp.concatenate([k_in[...], v_in[...]], axis=1)
+    kv[b, c, x, :half] = k_in[...]
+    kv[b, c, x, half:] = v_in[...]
     pl.semaphore_wait(barrier, num_blocks + 1)
 
     def z_gather(d):
-        mine = kv.at[b, c, x]
-        return remote(mine, mine, zs.at[d], zr.at[d], (2 * (b + d) + c, head))
+        piece = kv.at[b - d, c, x]
+        return remote(piece, piece, zs.at[d], zr.at[d + 1], (2 * (b + 1) + c, head))
 
     def z_arrival(d):
         piece = kv.at[b - d, c, x]
-        return remote(piece, piece, zs.at[d], zr.at[d], (2 * (b - d) + c, head))
+        return remote(piece, piece, zs.at[d], zr.at[d], (2 * (b - 1) + c, head))
 
     def x_gather(d, side):
         piece = kv.at[b - d, c, side]
@@ -78,10 +79,9 @@
         return remote(piece, piece, cs.at[d, which], cr.at[d, which], core_dev)
 
     x_gather(0, x).start()
-    for d in reversed(range(1, num_blocks)):
-        @pl.when(b + d < num_blocks)
-        def _():
-            z_gather(d).start()
+    @pl.when(b + 1 < num_blocks)
+    def _():
+        z_gather(0).start()
     core_gather(0, 0, c).start()
 
     def forward_z(d):
@@ -89,6 +89,10 @@
         def _():
             z_arrival(d).wait_recv()
             x_gather(d, x).start()
+            if d + 1 < num_blocks:
+                @pl.when(b + 1 < num_blocks)
+                def _():
+                    z_gather(d).start()
             core_gather(d, 0, c).start()
 
     def forward_x(d):
@@ -107,15 +111,16 @@
     low_lanes = lane < half
 
     def tiles(block):
-        left = jnp.concatenate([kv[block, 0, 0], kv[block, 1, 0]], axis=0).astype(F32)
-        right = jnp.concatenate([kv[block, 0, 1], kv[block, 1, 1]], axis=0).astype(F32)
-        keys = jnp.where(low_lanes, left, pltpu.roll(right, half, 1))
-        values = jnp.where(low_lanes, pltpu.roll(left, half, 1), right)
+        wide = [jnp.concatenate([kv[block, 0, side], kv[block, 1, side]], axis=1) for side in range(2)]
+        keys = jnp.concatenate([wide[0][:half], wide[1][:half]], axis=0)
+        values = jnp.concatenate([wide[0][half:], wide[1][half:]], axis=0)
         return keys, values
 
-    def first_pass(slot, keys, values, usable):
-        key_low, value_low = keys.astype(BF16), values.astype(BF16)
-        for h in range(heads):
+    def first_pass(slot, tiles, usable, which):
+        key_low, value_low = (tile.astype(F32).T.astype(BF16) for tile in tiles)
+        at = pl.ds(slot * BLOCK, BLOCK)
+        k_t[:, at], v_t[:, at] = tiles
+        for h in which:
             s = dot(key_low, q4[h], (1, 1))
             if slot == 0:
                 place = lax.broadcasted_iota(jnp.int32, (BLOCK, rows), 0)
@@ -129,29 +134,36 @@
             top[slot, h] = m if slot == 0 else jnp.where(usable, m, NEGATIVE)
             total[slot, h] = jnp.sum(e, axis=0, keepdims=True)
             prod[slot, h] = jnp.sum(e * dp, axis=0, keepdims=True)
-        at = pl.ds(slot * BLOCK, BLOCK)
-        k_t[:, at] = keys.T.astype(BF16)
-        v_t[:, at] = values.T.astype(BF16)
-
+
+    every = list(range(heads))
+    early, late = every[: heads // 2], every[heads // 2 :]
     forward_x(0)
-    if num_blocks > 1:
-        forward_z(1)
+    for d in range(1, min(3, num_blocks)):
+        forward_z(d)
+        if d == 1:
+            forward_x(d)
     for load in loads:
         load.wait()
     settle(0)
-    first_pass(0, *tiles(b), None)
-    for d in range(2, num_blocks):
+    own_tiles = tiles(b)
+    first_pass(0, own_tiles, None, early)
+    if num_blocks > 2:
+        forward_x(2)
+    if num_blocks > 3:
+        forward_z(3)
+    first_pass(0, own_tiles, None, late)
+    if num_blocks > 3:
+        forward_x(3)
+    for d in range(4, num_blocks):
         forward_z(d)
-        forward_x(d - 1)
-    if num_blocks > 1:
-        forward_x(num_blocks - 1)
+        forward_x(d)
     for d in range(1, num_blocks):
         settle(d)
 
-    offsets = [None] + [picks[b, group, j] for j in range(chosen - 1)]
+    offsets = [None] + [picks[group, j, b] for j in range(chosen - 1)]
     for slot in range(1, chosen):
         wanted = b - offsets[slot]
-        first_pass(slot, *tiles(jnp.maximum(wanted, 0)), wanted >= 0)
+        first_pass(slot, tiles(jnp.maximum(wanted, 0)), wanted >= 0, every)
 
     shares, deltas = [], []
     for h in range(heads):
@@ -170,10 +182,10 @@
     def x_return(slot):
         return remote(x_out.at[slot], x_in.at[slot], xs2.at[slot], xr2.at[slot], x_dev)
 
-    def second_pass(slot):
+    def second_pass(slot, which, before=None):
         at = pl.ds(slot * BLOCK, BLOCK)
-        grad_k = grad_v = None
-        for h in range(heads):
+        grad_k, grad_v = before or (None, None)
+        for h in which:
             probs = ev[slot, h] * shares[h][slot]
             low = probs.astype(BF16)
             ds = (probs * (dpv[slot, h] - deltas[h])).astype(BF16)
@@ -183,6 +195,10 @@
             more_k = dot(ds, q4[h], (1, 0))
             grad_v = more_v if grad_v is None else grad_v + more_v
             grad_k = more_k if grad_k is None else grad_k + more_k
+        return grad_k, grad_v
+
+    def hand_over(slot, grads):
+        grad_k, grad_v = grads
         grad_k = grad_k * scaling
         left = jnp.where(low_lanes, grad_k, pltpu.roll(grad_v, half, 1)).astype(BF16)
         right = jnp.where(low_lanes, pltpu.roll(grad_k, half, 1), grad_v).astype(BF16)
@@ -205,13 +221,13 @@
     def z_return(d):
         return remote(z_out.at[d], z_in.at[d], zs2.at[d], zr2.at[d], (2 * (b - d) + c, head))
 
-    second_pass(1)
-    for slot in range(2, chosen):
-        second_pass(slot)
-        cross(slot - 1)
-    second_pass(0)
+    for slot in range(1, chosen):
+        hand_over(slot, second_pass(slot, every))
+        if slot > 1:
+            cross(slot - 1)
+    grads = second_pass(0, early)
     cross(chosen - 1)
-    cross(0)
+    hand_over(0, second_pass(0, late, grads))
     for slot in range(1, chosen):
         land(slot)
     for d in reversed(range(1, num_blocks)):
@@ -221,6 +237,7 @@
                 jnp.where(offsets[slot] == d, summed[slot], 0.0) for slot in range(1, chosen)
             ).astype(BF16)
             z_return(d).start()
+    cross(0)
 
     stores = []
     for h in range(heads):
@@ -238,9 +255,7 @@
         def _():
             z_return(d).wait_recv()
             summed[0] = summed[0] + z_in[d].astype(F32)
-    owned = summed[0]
-    dk_out[...] = owned[:, :half]
-    dv_out[...] = owned[:, half:]
+    grads_out[...] = summed[0].T
 
     for store in stores:
         store.wait()
@@ -250,16 +265,31 @@
             x_gather(d, x).wait_send()
             core_gather(d, 0, c).wait_send()
             core_gather(d, 1, c).wait_send()
+    for d in range(num_blocks - 1):
+        @pl.when((d <= b) & (b + 1 < num_blocks))
+        def _():
+            z_gather(d).wait_send()
     for d in range(1, num_blocks):
-        @pl.when(b + d < num_blocks)
-        def _():
-            z_gather(d).wait_send()
         @pl.when(d <= b)
         def _():
             z_return(d).wait_send()
     for slot in range(chosen):
         core_return(slot).wait_send()
         x_return(slot).wait_send()
+
+
+def settle_outputs(attn, dq, grads, attn_out, dq_out, dk_out, dv_out, sem):
+    rows, half = attn.shape[0], dk_out.shape[0]
+    moves = [(grads.at[pl.ds(0, half)], dk_out), (grads.at[pl.ds(half, half)], dv_out)]
+    cut = rows // 4
+    for i in range(4):
+        at = pl.ds(i * cut, cut)
+        moves += [(attn.at[at], attn_out.at[at]), (dq.at[at], dq_out.at[at])]
+    copies = [pltpu.make_async_copy(src, dst, sem.at[i]) for i, (src, dst) in enumerate(moves)]
+    for copy in copies:
+        copy.start()
+    for copy in copies:
+        copy.wait()
 
 
 def local(queries, key_states, value_states, block_picks, grad_output):
@@ -274,18 +304,17 @@
     vmem = pl.BlockSpec(memory_space=pltpu.VMEM)
     anywhere = pl.BlockSpec(memory_space=pl.ANY)
     dma = pltpu.SemaphoreType.DMA
-    return pl.pallas_call(
+    attn, dq, grads = pl.pallas_call(
         functools.partial(kernel, seq_size, chosen),
         out_shape=(
             jax.ShapeDtypeStruct(queries.shape, BF16),
             jax.ShapeDtypeStruct(queries.shape, F32),
-            jax.ShapeDtypeStruct(key_states.shape, F32),
-            jax.ShapeDtypeStruct(value_states.shape, F32),
+            jax.ShapeDtypeStruct((dim, rows), F32),
         ),
         in_specs=[pl.BlockSpec(memory_space=pltpu.SMEM), vmem, vmem, anywhere, anywhere],
-        out_specs=(anywhere, anywhere, vmem, vmem),
+        out_specs=(anywhere, anywhere, vmem),
         scratch_shapes=[
-            pltpu.VMEM((num_blocks, 2, 2, rows, dim), BF16),
+            pltpu.VMEM((num_blocks, 2, 2, dim, rows), BF16),
             pltpu.VMEM((heads, rows, dim), BF16),
             pltpu.VMEM((heads, rows, dim), BF16),
             pltpu.VMEM((chosen, heads, BLOCK, rows), F32),
@@ -327,7 +356,21 @@
         cost_estimate=pl.CostEstimate(
             flops=10 * heads * rows * keys * dim, bytes_accessed=4 * queries.size * 4, transcendentals=heads * rows * keys
         ),
-    )(block_picks, key_states, value_states, queries, grad_output)
+    )(block_picks.transpose(1, 2, 0), key_states.T, value_states.T, queries, grad_output)
+    attn, dq, dk, dv = pl.pallas_call(
+        settle_outputs,
+        out_shape=(
+            jax.ShapeDtypeStruct(attn.shape, attn.dtype),
+            jax.ShapeDtypeStruct(dq.shape, dq.dtype),
+            jax.ShapeDtypeStruct((half, rows), F32),
+            jax.ShapeDtypeStruct((half, rows), F32),
+        ),
+        in_specs=[anywhere] * 3,
+        out_specs=(anywhere,) * 4,
+        scratch_shapes=[dma((10,))],
+        cost_estimate=pl.CostEstimate(flops=0, bytes_accessed=2 * 7 * queries.size, transcendentals=0),
+    )(attn, dq, grads)
+    return attn, dq, dk.T, dv.T
 
 
 def solution(mesh):

time: 44.9 us -> 65.2 us (1.45)
  Pallas kernels: 34.6 us -> 64.4 us
  local copies, waits for them, and re-layouts: 9.35 us -> 0 us
    pallas_call x0 -> x1, Pallas kernels: none -> 29 us  [local(): pl.pallas_call(settle_outputs, out_shape=(jax.ShapeDtypeStruct(attn.shape...]
    unnamed x9 -> x0, local copies, waits for them, and re-layouts: 6.06 us -> none
    pallas_call x2 -> x0, local copies, waits for them, and re-layouts: 3.29 us -> none  [local(): pl.pallas_call(functools.partial(kernel, seq_size, chosen), out_shape=(ja...]
    pallas_call x1, Pallas kernels: 34.6 us -> 35.4 us  [local(): pl.pallas_call(functools.partial(kernel, seq_size, chosen), out_shape=(ja...]
where the time goes in v2:
time: 65.2 us; the launch traced here: 65 us
  Pallas kernels  64.4 us (99%)
    pallas_call x1, Pallas kernels, local(): pl.pallas_call(functools.partial(kernel, seq_size, chosen), out_shape=(ja...  35.4 us
    pallas_call x1, Pallas kernels, local(): pl.pallas_call(settle_outputs, out_shape=(jax.ShapeDtypeStruct(attn.shape...  29 us

profile of v2, /device:TPU:0, one launch (start us, length us, event | category | flops | bytes accessed | tf_op | source)
XLA Modules:
  0.0 65.0 jit_solution(6196889567215326061)
XLA Ops:
  0.6 35.4 %shard_map.84 = (bf16[256,512]{1,0:T(8,128)(2,1)}, f32[256,512]{1,0:T(8,128)}, f32[128,256]{1,0:T(8,128)}) custom-call(s32[2,2,4]{2,1,0:T(2,128)} %bitcast.9, bf16[64,256]{1,0:T(8,128)(2,1)} %bitcast.7, bf16[64,256]{1,0:T(8,128)(2,1)} %bitcast.8, bf16[256,512]{1,0:T(8,128)(2,1)} %q_hbm.1, bf16[256,512]{1,0:T(8,128)(2,1)} %g_hbm.1), custom_call_target="tpu_custom_call" | custom-call | flops 2013265920 | bytes 2097152 | tf_op jit(solution)/shard_map/pallas_call | solution.py:307
  36.1 29.0 %shard_map.85 = (bf16[256,512]{1,0:T(8,128)(2,1)}, f32[256,512]{1,0:T(8,128)}, f32[64,256]{1,0:T(8,128)}, f32[64,256]{1,0:T(8,128)}) custom-call(bf16[256,512]{1,0:T(8,128)(2,1)} %get-tuple-element.11.attn, f32[256,512]{1,0:T(8,128)} %get-tuple-element.12.dq, f32[128,256]{1,0:T(8,128)} %get-tuple-element.13.grads), custom_call_target="tpu_custom_call" | custom-call | bytes 1835008 | tf_op jit(solution)/shard_map/pallas_call | solution.py:360

commit v3 on v2

--- a/solution.py
+++ b/solution.py
@@ -21,7 +21,7 @@
 
 def kernel(
     seq_size, chosen, picks, k_in, v_in, q_hbm, g_hbm, attn_hbm, dq_hbm, grads_out,
-    kv, q4, g4, ev, dpv, p_low, ds_low, k_t, v_t, top, total, prod, attn_buf, dq_buf,
+    kv, q4, g4, k_low, v_low, ev, dpv, p_low, ds_low, k_t, v_t, top, total, prod, attn_buf, dq_buf,
     part, core_in, x_out, x_in, summed, z_out, z_in,
     in_sem, out_sem, zs, zr, xs, xr, cs, cr, cs2, cr2, xs2, xr2, zs2, zr2,
 ):
@@ -116,27 +116,34 @@
         values = jnp.concatenate([wide[0][half:], wide[1][half:]], axis=0)
         return keys, values
 
-    def first_pass(slot, tiles, usable, which):
-        key_low, value_low = (tile.astype(F32).T.astype(BF16) for tile in tiles)
-        at = pl.ds(slot * BLOCK, BLOCK)
-        k_t[:, at], v_t[:, at] = tiles
-        for h in which:
-            s = dot(key_low, q4[h], (1, 1))
-            if slot == 0:
-                place = lax.broadcasted_iota(jnp.int32, (BLOCK, rows), 0)
-                query = lax.broadcasted_iota(jnp.int32, (BLOCK, rows), 1) + c * rows
-                s = jnp.where(place <= query, s, NEGATIVE)
-            m = jnp.max(s, axis=0, keepdims=True)
-            e = jnp.exp2((s - m) * rate)
-            dp = dot(value_low, g4[h], (1, 1))
-            ev[slot, h] = e
-            dpv[slot, h] = dp
-            top[slot, h] = m if slot == 0 else jnp.where(usable, m, NEGATIVE)
-            total[slot, h] = jnp.sum(e, axis=0, keepdims=True)
-            prod[slot, h] = jnp.sum(e * dp, axis=0, keepdims=True)
-
-    every = list(range(heads))
-    early, late = every[: heads // 2], every[heads // 2 :]
+    def prepare(slot, block):
+        key_tile, value_tile = tiles(block)
+        at = pl.ds(pl.multiple_of(slot * BLOCK, BLOCK), BLOCK)
+        k_t[:, at] = key_tile
+        v_t[:, at] = value_tile
+        k_low[slot] = key_tile.astype(F32).T.astype(BF16)
+        v_low[slot] = value_tile.astype(F32).T.astype(BF16)
+
+    def first_pass(slot, h, usable, causal):
+        s = dot(k_low[slot], q4[h], (1, 1))
+        if causal:
+            place = lax.broadcasted_iota(jnp.int32, (BLOCK, rows), 0)
+            query = lax.broadcasted_iota(jnp.int32, (BLOCK, rows), 1) + c * rows
+            s = jnp.where(place <= query, s, NEGATIVE)
+        dp = dot(v_low[slot], g4[h], (1, 1))
+        m = jnp.max(s, axis=0, keepdims=True)
+        e = jnp.exp2((s - m) * rate)
+        ev[slot, h] = e
+        dpv[slot, h] = dp
+        top[slot, h] = m if causal else jnp.where(usable, m, NEGATIVE)
+        total[slot, h] = jnp.sum(e, axis=0, keepdims=True)
+        prod[slot, h] = jnp.sum(e * dp, axis=0, keepdims=True)
+
+    def own_heads(start, stop):
+        @pl.loop(start, stop)
+        def _(h):
+            first_pass(0, h, None, True)
+
     forward_x(0)
     for d in range(1, min(3, num_blocks)):
         forward_z(d)
@@ -145,13 +152,13 @@
     for load in loads:
         load.wait()
     settle(0)
-    own_tiles = tiles(b)
-    first_pass(0, own_tiles, None, early)
+    prepare(0, b)
+    own_heads(0, heads // 2)
     if num_blocks > 2:
         forward_x(2)
     if num_blocks > 3:
         forward_z(3)
-    first_pass(0, own_tiles, None, late)
+    own_heads(heads // 2, heads)
     if num_blocks > 3:
         forward_x(3)
     for d in range(4, num_blocks):
@@ -163,18 +170,23 @@
     offsets = [None] + [picks[group, j, b] for j in range(chosen - 1)]
     for slot in range(1, chosen):
         wanted = b - offsets[slot]
-        first_pass(slot, tiles(jnp.maximum(wanted, 0)), wanted >= 0, every)
-
-    shares, deltas = [], []
-    for h in range(heads):
+        prepare(slot, jnp.maximum(wanted, 0))
+
+        @pl.loop(0, heads)
+        def _(h):
+            first_pass(slot, h, wanted >= 0, False)
+
+    @pl.loop(0, heads)
+    def _(h):
         m = top[0, h]
         for slot in range(1, chosen):
             m = jnp.maximum(m, top[slot, h])
         weight = [jnp.exp2((top[slot, h] - m) * rate) for slot in range(chosen)]
         norm = sum(weight[slot] * total[slot, h] for slot in range(chosen))
         share = [w / norm for w in weight]
-        shares.append(share)
-        deltas.append(sum(share[slot] * prod[slot, h] for slot in range(chosen)))
+        for slot in range(chosen):
+            top[slot, h] = share[slot]
+        total[0, h] = sum(share[slot] * prod[slot, h] for slot in range(chosen))
 
     def core_return(slot):
         return remote(part.at[slot, oc], core_in.at[slot], cs2.at[slot], cr2.at[slot], core_dev)
@@ -182,24 +194,20 @@
     def x_return(slot):
         return remote(x_out.at[slot], x_in.at[slot], xs2.at[slot], xr2.at[slot], x_dev)
 
-    def second_pass(slot, which, before=None):
-        at = pl.ds(slot * BLOCK, BLOCK)
-        grad_k, grad_v = before or (None, None)
-        for h in which:
-            probs = ev[slot, h] * shares[h][slot]
-            low = probs.astype(BF16)
-            ds = (probs * (dpv[slot, h] - deltas[h])).astype(BF16)
-            p_low[h, at] = low
-            ds_low[h, at] = ds
-            more_v = dot(low, g4[h], (1, 0))
-            more_k = dot(ds, q4[h], (1, 0))
-            grad_v = more_v if grad_v is None else grad_v + more_v
-            grad_k = more_k if grad_k is None else grad_k + more_k
-        return grad_k, grad_v
-
-    def hand_over(slot, grads):
-        grad_k, grad_v = grads
-        grad_k = grad_k * scaling
+    def second_pass(slot):
+        at = pl.ds(pl.multiple_of(slot * BLOCK, BLOCK), BLOCK)
+
+        @pl.loop(0, heads)
+        def _(h):
+            cols = pl.ds(pl.multiple_of(h * rows, rows), rows)
+            probs = ev[slot, h] * top[slot, h]
+            p_low[at, cols] = probs.astype(BF16)
+            ds_low[at, cols] = (probs * (dpv[slot, h] - total[0, h])).astype(BF16)
+
+    def hand_over(slot):
+        at = pl.ds(pl.multiple_of(slot * BLOCK, BLOCK), BLOCK)
+        grad_v = dot(p_low[at], g4[...].reshape(heads * rows, dim), (1, 0))
+        grad_k = dot(ds_low[at], q4[...].reshape(heads * rows, dim), (1, 0)) * scaling
         left = jnp.where(low_lanes, grad_k, pltpu.roll(grad_v, half, 1)).astype(BF16)
         right = jnp.where(low_lanes, pltpu.roll(grad_k, half, 1), grad_v).astype(BF16)
         for side in range(2):
@@ -221,13 +229,17 @@
     def z_return(d):
         return remote(z_out.at[d], z_in.at[d], zs2.at[d], zr2.at[d], (2 * (b - d) + c, head))
 
-    for slot in range(1, chosen):
-        hand_over(slot, second_pass(slot, every))
-        if slot > 1:
-            cross(slot - 1)
-    grads = second_pass(0, early)
-    cross(chosen - 1)
-    hand_over(0, second_pass(0, late, grads))
+    @pl.loop(0, chosen)
+    def _(step):
+        slot = lax.rem(step + 1, chosen)
+        second_pass(slot)
+
+        @pl.when(step > 0)
+        def _():
+            cross(step)
+
+        hand_over(slot)
+
     for slot in range(1, chosen):
         land(slot)
     for d in reversed(range(1, num_blocks)):
@@ -239,13 +251,13 @@
             z_return(d).start()
     cross(0)
 
+    attn_buf[...] = dot(v_t[...], p_low[...], (1, 0)).T.astype(BF16)
+    dq_buf[...] = (dot(k_t[...], ds_low[...], (1, 0)) * scaling).T
     stores = []
     for h in range(heads):
-        attn_buf[h] = dot(v_t[...], p_low[h], (1, 0)).T.astype(BF16)
-        dq_buf[h] = dot(k_t[...], ds_low[h], (1, 0)).T * scaling
-        cols = pl.ds(h * dim, dim)
-        stores.append(pltpu.make_async_copy(attn_buf.at[h], attn_hbm.at[:, cols], out_sem.at[0, h]))
-        stores.append(pltpu.make_async_copy(dq_buf.at[h], dq_hbm.at[:, cols], out_sem.at[1, h]))
+        at, cols = pl.ds(h * rows, rows), pl.ds(h * dim, dim)
+        stores.append(pltpu.make_async_copy(attn_buf.at[at], attn_hbm.at[:, cols], out_sem.at[0, h]))
+        stores.append(pltpu.make_async_copy(dq_buf.at[at], dq_hbm.at[:, cols], out_sem.at[1, h]))
         stores[-2].start()
         stores[-1].start()
 
@@ -278,17 +290,25 @@
         x_return(slot).wait_send()
 
 
-def settle_outputs(attn, dq, grads, attn_out, dq_out, dk_out, dv_out, sem):
+def settle_outputs(attn, dq, grads, attn_out, dq_out, dk_out, dv_out, attn_buf, dq_buf, grads_buf, sem):
     rows, half = attn.shape[0], dk_out.shape[0]
-    moves = [(grads.at[pl.ds(0, half)], dk_out), (grads.at[pl.ds(half, half)], dv_out)]
-    cut = rows // 4
-    for i in range(4):
+    cut = rows // 2
+    moves = []
+    for i in range(2):
         at = pl.ds(i * cut, cut)
-        moves += [(attn.at[at], attn_out.at[at]), (dq.at[at], dq_out.at[at])]
-    copies = [pltpu.make_async_copy(src, dst, sem.at[i]) for i, (src, dst) in enumerate(moves)]
-    for copy in copies:
+        moves.append((dq.at[at], dq_buf.at[at], dq_out.at[at]))
+        moves.append((attn.at[at], attn_buf.at[at], attn_out.at[at]))
+    for i, out in enumerate((dk_out, dv_out)):
+        at = pl.ds(i * half, half)
+        moves.append((grads.at[at], grads_buf.at[at], out))
+    arrive = [pltpu.make_async_copy(src, mid, sem.at[0, i]) for i, (src, mid, _) in enumerate(moves)]
+    leave = [pltpu.make_async_copy(mid, dst, sem.at[1, i]) for i, (_, mid, dst) in enumerate(moves)]
+    for copy in arrive:
         copy.start()
-    for copy in copies:
+    for first, then in zip(arrive, leave):
+        first.wait()
+        then.start()
+    for copy in leave:
         copy.wait()
 
 
@@ -317,17 +337,19 @@
             pltpu.VMEM((num_blocks, 2, 2, dim, rows), BF16),
             pltpu.VMEM((heads, rows, dim), BF16),
             pltpu.VMEM((heads, rows, dim), BF16),
+            pltpu.VMEM((chosen, BLOCK, dim), BF16),
+            pltpu.VMEM((chosen, BLOCK, dim), BF16),
             pltpu.VMEM((chosen, heads, BLOCK, rows), F32),
             pltpu.VMEM((chosen, heads, BLOCK, rows), F32),
-            pltpu.VMEM((heads, keys, rows), BF16),
-            pltpu.VMEM((heads, keys, rows), BF16),
+            pltpu.VMEM((keys, heads * rows), BF16),
+            pltpu.VMEM((keys, heads * rows), BF16),
             pltpu.VMEM((dim, keys), BF16),
             pltpu.VMEM((dim, keys), BF16),
             pltpu.VMEM((chosen, heads, 1, rows), F32),
             pltpu.VMEM((chosen, heads, 1, rows), F32),
             pltpu.VMEM((chosen, heads, 1, rows), F32),
-            pltpu.VMEM((heads, rows, dim), BF16),
-            pltpu.VMEM((heads, rows, dim), F32),
+            pltpu.VMEM((heads * rows, dim), BF16),
+            pltpu.VMEM((heads * rows, dim), F32),
             pltpu.VMEM((chosen, 2, 2, rows, dim), BF16),
             pltpu.VMEM((chosen, 2, rows, dim), BF16),
             pltpu.VMEM((chosen, rows, dim), BF16),
@@ -367,7 +389,12 @@
         ),
         in_specs=[anywhere] * 3,
         out_specs=(anywhere,) * 4,
-        scratch_shapes=[dma((10,))],
+        scratch_shapes=[
+            pltpu.VMEM(attn.shape, attn.dtype),
+            pltpu.VMEM(dq.shape, dq.dtype),
+            pltpu.VMEM(grads.shape, grads.dtype),
+            dma((2, 6)),
+        ],
         cost_estimate=pl.CostEstimate(flops=0, bytes_accessed=2 * 7 * queries.size, transcendentals=0),
     )(attn, dq, grads)
     return attn, dq, dk.T, dv.T

time: 65.2 us -> 40.8 us (0.63)
  Pallas kernels: 64.4 us -> 39.9 us
    pallas_call x1, Pallas kernels: 29 us -> 1.98 us  [local(): pl.pallas_call(settle_outputs, out_shape=(jax.ShapeDtypeStruct(attn.shape...]
    pallas_call x1, Pallas kernels: 35.4 us -> 37.9 us  [local(): pl.pallas_call(functools.partial(kernel, seq_size, chosen), out_shape=(ja...]
where the time goes in v3:
time: 40.8 us; the launch traced here: 40.6 us
  Pallas kernels  39.9 us (98%)
  between operations  0.64 us (2%)
    pallas_call x1, Pallas kernels, local(): pl.pallas_call(functools.partial(kernel, seq_size, chosen), out_shape=(ja...  37.9 us
    pallas_call x1, Pallas kernels, local(): pl.pallas_call(settle_outputs, out_shape=(jax.ShapeDtypeStruct(attn.shape...  1.98 us

profile of v3, /device:TPU:0, one launch (start us, length us, event | category | flops | bytes accessed | tf_op | source)
XLA Modules:
  0.0 40.6 jit_solution(10678205299341524146)
XLA Ops:
  0.6 37.9 %shard_map.84 = (bf16[256,512]{1,0:T(8,128)(2,1)}, f32[256,512]{1,0:T(8,128)}, f32[128,256]{1,0:T(8,128)}) custom-call(s32[2,2,4]{2,1,0:T(2,128)} %bitcast.9, bf16[64,256]{1,0:T(8,128)(2,1)} %bitcast.7, bf16[64,256]{1,0:T(8,128)(2,1)} %bitcast.8, bf16[256,512]{1,0:T(8,128)(2,1)} %q_hbm.1, bf16[256,512]{1,0:T(8,128)(2,1)} %g_hbm.1), custom_call_target="tpu_custom_call" | custom-call | flops 2013265920 | bytes 2097152 | tf_op jit(solution)/shard_map/pallas_call | solution.py:327
  38.6 2.0 %shard_map.85 = (bf16[256,512]{1,0:T(8,128)(2,1)}, f32[256,512]{1,0:T(8,128)}, f32[64,256]{1,0:T(8,128)}, f32[64,256]{1,0:T(8,128)}) custom-call(bf16[256,512]{1,0:T(8,128)(2,1)} %get-tuple-element.11.attn, f32[256,512]{1,0:T(8,128)} %get-tuple-element.12.dq, f32[128,256]{1,0:T(8,128)} %get-tuple-element.13.grads), custom_call_target="tpu_custom_call" | custom-call | bytes 1835008 | tf_op jit(solution)/shard_map/pallas_call | solution.py:382

commit v4 on v3

--- a/solution.py
+++ b/solution.py
@@ -38,6 +38,7 @@
     x_dev = (seq, 2 * group + ox)
     scaling = dim ** (-0.5)
     rate = scaling * LOG2E
+    part_rows = rows // 2
 
     def remote(src, dst, send, recv, dev):
         return pltpu.make_async_remote_copy(
@@ -107,9 +108,6 @@
             core_gather(d, 0, oc).wait_recv()
             core_gather(d, 1, oc).wait_recv()
 
-    lane = lax.broadcasted_iota(jnp.int32, (BLOCK, dim), 1)
-    low_lanes = lane < half
-
     def tiles(block):
         wide = [jnp.concatenate([kv[block, 0, side], kv[block, 1, side]], axis=1) for side in range(2)]
         keys = jnp.concatenate([wide[0][:half], wide[1][:half]], axis=0)
@@ -118,32 +116,36 @@
 
     def prepare(slot, block):
         key_tile, value_tile = tiles(block)
-        at = pl.ds(pl.multiple_of(slot * BLOCK, BLOCK), BLOCK)
-        k_t[:, at] = key_tile
-        v_t[:, at] = value_tile
+        for piece in range(4):
+            side, chunk = piece % 2, piece // 2
+            cut = slice(side * rows + chunk * part_rows, side * rows + (chunk + 1) * part_rows)
+            at = pl.ds(pl.multiple_of(slot * BLOCK + piece * part_rows, part_rows), part_rows)
+            k_t[:, at] = key_tile[:, cut]
+            v_t[:, at] = value_tile[:, cut]
         k_low[slot] = key_tile.astype(F32).T.astype(BF16)
         v_low[slot] = value_tile.astype(F32).T.astype(BF16)
 
-    def first_pass(slot, h, usable, causal):
-        s = dot(k_low[slot], q4[h], (1, 1))
-        if causal:
-            place = lax.broadcasted_iota(jnp.int32, (BLOCK, rows), 0)
-            query = lax.broadcasted_iota(jnp.int32, (BLOCK, rows), 1) + c * rows
-            s = jnp.where(place <= query, s, NEGATIVE)
-        dp = dot(v_low[slot], g4[h], (1, 1))
-        m = jnp.max(s, axis=0, keepdims=True)
-        e = jnp.exp2((s - m) * rate)
-        ev[slot, h] = e
-        dpv[slot, h] = dp
-        top[slot, h] = m if causal else jnp.where(usable, m, NEGATIVE)
-        total[slot, h] = jnp.sum(e, axis=0, keepdims=True)
-        prod[slot, h] = jnp.sum(e * dp, axis=0, keepdims=True)
-
-    def own_heads(start, stop):
-        @pl.loop(start, stop)
-        def _(h):
-            first_pass(0, h, None, True)
-
+    def first_pass(slot, which, usable, causal):
+        for h in which:
+            s = dot(k_low[slot], q4[h], (1, 1))
+            if causal:
+                place = lax.broadcasted_iota(jnp.int32, (BLOCK, rows), 0)
+                query = lax.broadcasted_iota(jnp.int32, (BLOCK, rows), 1) + c * rows
+                s = jnp.where(place <= query, s, NEGATIVE)
+            dp = dot(v_low[slot], g4[h], (1, 1))
+            m = jnp.max(s, axis=0, keepdims=True)
+            e = jnp.exp2((s - m) * rate)
+            for piece in range(4):
+                side, chunk = piece % 2, piece // 2
+                cut = slice(side * rows + chunk * part_rows, side * rows + (chunk + 1) * part_rows)
+                at = slice(side * part_rows, (side + 1) * part_rows)
+                ev[2 * slot + chunk, h, at] = e[cut]
+                dpv[2 * slot + chunk, h, at] = dp[cut]
+            top[slot, h] = m if causal else jnp.where(usable, m, NEGATIVE)
+            total[slot, h] = jnp.sum(e, axis=0, keepdims=True)
+            prod[slot, h] = jnp.sum(e * dp, axis=0, keepdims=True)
+
+    every = list(range(heads))
     forward_x(0)
     for d in range(1, min(3, num_blocks)):
         forward_z(d)
@@ -153,12 +155,12 @@
         load.wait()
     settle(0)
     prepare(0, b)
-    own_heads(0, heads // 2)
+    first_pass(0, every[: heads // 2], None, True)
     if num_blocks > 2:
         forward_x(2)
     if num_blocks > 3:
         forward_z(3)
-    own_heads(heads // 2, heads)
+    first_pass(0, every[heads // 2 :], None, True)
     if num_blocks > 3:
         forward_x(3)
     for d in range(4, num_blocks):
@@ -168,16 +170,13 @@
         settle(d)
 
     offsets = [None] + [picks[group, j, b] for j in range(chosen - 1)]
-    for slot in range(1, chosen):
-        wanted = b - offsets[slot]
+    @pl.loop(1, chosen)
+    def _(slot):
+        wanted = b - picks[group, slot - 1, b]
         prepare(slot, jnp.maximum(wanted, 0))
-
-        @pl.loop(0, heads)
-        def _(h):
-            first_pass(slot, h, wanted >= 0, False)
-
-    @pl.loop(0, heads)
-    def _(h):
+        first_pass(slot, every, wanted >= 0, False)
+
+    for h in every:
         m = top[0, h]
         for slot in range(1, chosen):
             m = jnp.maximum(m, top[slot, h])
@@ -188,68 +187,83 @@
             top[slot, h] = share[slot]
         total[0, h] = sum(share[slot] * prod[slot, h] for slot in range(chosen))
 
-    def core_return(slot):
-        return remote(part.at[slot, oc], core_in.at[slot], cs2.at[slot], cr2.at[slot], core_dev)
-
-    def x_return(slot):
-        return remote(x_out.at[slot], x_in.at[slot], xs2.at[slot], xr2.at[slot], x_dev)
-
-    def second_pass(slot):
-        at = pl.ds(pl.multiple_of(slot * BLOCK, BLOCK), BLOCK)
-
-        @pl.loop(0, heads)
-        def _(h):
-            cols = pl.ds(pl.multiple_of(h * rows, rows), rows)
-            probs = ev[slot, h] * top[slot, h]
-            p_low[at, cols] = probs.astype(BF16)
-            ds_low[at, cols] = (probs * (dpv[slot, h] - total[0, h])).astype(BF16)
-
-    def hand_over(slot):
-        at = pl.ds(pl.multiple_of(slot * BLOCK, BLOCK), BLOCK)
-        grad_v = dot(p_low[at], g4[...].reshape(heads * rows, dim), (1, 0))
-        grad_k = dot(ds_low[at], q4[...].reshape(heads * rows, dim), (1, 0)) * scaling
-        left = jnp.where(low_lanes, grad_k, pltpu.roll(grad_v, half, 1)).astype(BF16)
-        right = jnp.where(low_lanes, pltpu.roll(grad_k, half, 1), grad_v).astype(BF16)
+    def core_return(unit):
+        return remote(part.at[unit, oc], core_in.at[unit], cs2.at[unit], cr2.at[unit], core_dev)
+
+    def x_return(unit):
+        return remote(x_out.at[unit], x_in.at[unit], xs2.at[unit], xr2.at[unit], x_dev)
+
+    def z_return(d, chunk):
+        return remote(
+            z_out.at[d, chunk], z_in.at[d, chunk], zs2.at[d, chunk], zr2.at[d, chunk], (2 * (b - d) + c, head)
+        )
+
+    def second_pass(unit):
+        slot = unit // 2
+        at = pl.ds(pl.multiple_of(unit * 2 * part_rows, 2 * part_rows), 2 * part_rows)
+        grad_k = grad_v = 0.0
+        for h in every:
+            cols = slice(h * rows, (h + 1) * rows)
+            probs = ev[unit, h] * top[slot, h]
+            low = probs.astype(BF16)
+            ds = (probs * (dpv[unit, h] - total[0, h])).astype(BF16)
+            p_low[at, cols] = low
+            ds_low[at, cols] = ds
+            grad_v += dot(low, g4[h], (1, 0))
+            grad_k += dot(ds, q4[h], (1, 0))
+        grad_k = grad_k * scaling
+        lanes = lax.broadcasted_iota(jnp.int32, grad_k.shape, 1) < half
+        left = jnp.where(lanes, grad_k, pltpu.roll(grad_v, half, 1)).astype(BF16)
+        right = jnp.where(lanes, pltpu.roll(grad_k, half, 1), grad_v).astype(BF16)
         for side in range(2):
-            cut = slice(side * rows, (side + 1) * rows)
-            part[slot, side, 0] = left[cut]
-            part[slot, side, 1] = right[cut]
-        core_return(slot).start()
-
-    def cross(slot):
-        core_return(slot).wait_recv()
-        x_out[slot] = (part[slot, c, ox].astype(F32) + core_in[slot, ox].astype(F32)).astype(BF16)
-        x_return(slot).start()
-        summed[slot] = part[slot, c, x].astype(F32) + core_in[slot, x].astype(F32)
-
-    def land(slot):
-        x_return(slot).wait_recv()
-        summed[slot] = summed[slot] + x_in[slot].astype(F32)
-
-    def z_return(d):
-        return remote(z_out.at[d], z_in.at[d], zs2.at[d], zr2.at[d], (2 * (b - d) + c, head))
-
-    @pl.loop(0, chosen)
+            cut = slice(side * part_rows, (side + 1) * part_rows)
+            part[unit, side, 0] = left[cut]
+            part[unit, side, 1] = right[cut]
+        core_return(unit).start()
+
+    def cross(unit):
+        core_return(unit).wait_recv()
+        x_out[unit] = (part[unit, c, ox].astype(F32) + core_in[unit, ox].astype(F32)).astype(BF16)
+        x_return(unit).start()
+        summed[unit] = part[unit, c, x].astype(F32) + core_in[unit, x].astype(F32)
+
+    def land(unit):
+        x_return(unit).wait_recv()
+        summed[unit] = summed[unit] + x_in[unit].astype(F32)
+
+    def send_back(chunk):
+        for slot in range(1, chosen):
+            land(2 * slot + chunk)
+        for d in reversed(range(1, num_blocks)):
+            @pl.when(d <= b)
+            def _():
+                z_out[d, chunk] = sum(
+                    jnp.where(picks[group, slot - 1, b] == d, summed[2 * slot + chunk], 0.0)
+                    for slot in range(1, chosen)
+                ).astype(BF16)
+                z_return(d, chunk).start()
+
+    others = chosen - 1
+
+    def unit_of(step):
+        tail = step // (2 * others)
+        slot = (1 - tail) * (1 + step % others)
+        return 2 * slot + (1 - tail) * (step // others) + tail * (step - 2 * others)
+
+    @pl.loop(0, 2 * chosen)
     def _(step):
-        slot = lax.rem(step + 1, chosen)
-        second_pass(slot)
+        second_pass(unit_of(step))
 
         @pl.when(step > 0)
         def _():
-            cross(step)
-
-        hand_over(slot)
-
-    for slot in range(1, chosen):
-        land(slot)
-    for d in reversed(range(1, num_blocks)):
-        @pl.when(d <= b)
-        def _():
-            z_out[d] = sum(
-                jnp.where(offsets[slot] == d, summed[slot], 0.0) for slot in range(1, chosen)
-            ).astype(BF16)
-            z_return(d).start()
-    cross(0)
+            cross(unit_of(step - 1))
+
+        @pl.when(step == 2 * others - 1)
+        def _():
+            send_back(0)
+
+    send_back(1)
+    cross(1)
 
     attn_buf[...] = dot(v_t[...], p_low[...], (1, 0)).T.astype(BF16)
     dq_buf[...] = (dot(k_t[...], ds_low[...], (1, 0)) * scaling).T
@@ -261,13 +275,15 @@
         stores[-2].start()
         stores[-1].start()
 
-    land(0)
-    for d in range(1, num_blocks):
-        @pl.when(b + d < num_blocks)
-        def _():
-            z_return(d).wait_recv()
-            summed[0] = summed[0] + z_in[d].astype(F32)
-    grads_out[...] = summed[0].T
+    for chunk in range(2):
+        land(chunk)
+        for d in range(1, num_blocks):
+            @pl.when(b + d < num_blocks)
+            def _():
+                z_return(d, chunk).wait_recv()
+                summed[chunk] = summed[chunk] + z_in[d, chunk].astype(F32)
+        at = pl.ds(chunk * part_rows, part_rows)
+        grads_out[:, at] = summed[chunk].T
 
     for store in stores:
         store.wait()
@@ -284,10 +300,11 @@
     for d in range(1, num_blocks):
         @pl.when(d <= b)
         def _():
-            z_return(d).wait_send()
-    for slot in range(chosen):
-        core_return(slot).wait_send()
-        x_return(slot).wait_send()
+            z_return(d, 0).wait_send()
+            z_return(d, 1).wait_send()
+    for unit in range(2 * chosen):
+        core_return(unit).wait_send()
+        x_return(unit).wait_send()
 
 
 def settle_outputs(attn, dq, grads, attn_out, dq_out, dk_out, dv_out, attn_buf, dq_buf, grads_buf, sem):
@@ -339,8 +356,8 @@
             pltpu.VMEM((heads, rows, dim), BF16),
             pltpu.VMEM((chosen, BLOCK, dim), BF16),
             pltpu.VMEM((chosen, BLOCK, dim), BF16),
-            pltpu.VMEM((chosen, heads, BLOCK, rows), F32),
-            pltpu.VMEM((chosen, heads, BLOCK, rows), F32),
+            pltpu.VMEM((2 * chosen, heads, rows, rows), F32),
+            pltpu.VMEM((2 * chosen, heads, rows, rows), F32),
             pltpu.VMEM((keys, heads * rows), BF16),
             pltpu.VMEM((keys, heads * rows), BF16),
             pltpu.VMEM((dim, keys), BF16),
@@ -350,13 +367,13 @@
             pltpu.VMEM((chosen, heads, 1, rows), F32),
             pltpu.VMEM((heads * rows, dim), BF16),
             pltpu.VMEM((heads * rows, dim), F32),
-            pltpu.VMEM((chosen, 2, 2, rows, dim), BF16),
-            pltpu.VMEM((chosen, 2, rows, dim), BF16),
-            pltpu.VMEM((chosen, rows, dim), BF16),
-            pltpu.VMEM((chosen, rows, dim), BF16),
-            pltpu.VMEM((chosen, rows, dim), F32),
-            pltpu.VMEM((num_blocks, rows, dim), BF16),
-            pltpu.VMEM((num_blocks, rows, dim), BF16),
+            pltpu.VMEM((2 * chosen, 2, 2, rows // 2, dim), BF16),
+            pltpu.VMEM((2 * chosen, 2, rows // 2, dim), BF16),
+            pltpu.VMEM((2 * chosen, rows // 2, dim), BF16),
+            pltpu.VMEM((2 * chosen, rows // 2, dim), BF16),
+            pltpu.VMEM((2 * chosen, rows // 2, dim), F32),
+            pltpu.VMEM((num_blocks, 2, rows // 2, dim), BF16),
+            pltpu.VMEM((num_blocks, 2, rows // 2, dim), BF16),
             dma((2, heads)),
             dma((2, heads)),
             dma((num_blocks,)),
@@ -365,12 +382,12 @@
             dma((num_blocks,)),
             dma((num_blocks, 2)),
             dma((num_blocks, 2)),
-            dma((chosen,)),
-            dma((chosen,)),
-            dma((chosen,)),
-            dma((chosen,)),
-            dma((num_blocks,)),
-            dma((num_blocks,)),
+            dma((2 * chosen,)),
+            dma((2 * chosen,)),
+            dma((2 * chosen,)),
+            dma((2 * chosen,)),
+            dma((num_blocks, 2)),
+            dma((num_blocks, 2)),
         ],
         compiler_params=pltpu.CompilerParams(
             collective_id=0, has_side_effects=True, vmem_limit_bytes=56 * 1024 * 1024

time: 40.8 us -> 39.5 us (0.968)
  Pallas kernels: 39.9 us -> 38.6 us
    pallas_call x1, Pallas kernels: 37.9 us -> 36.6 us  [local(): pl.pallas_call(functools.partial(kernel, seq_size, chosen), out_shape=(ja...]
where the time goes in v4:
time: 39.5 us; the launch traced here: 39.3 us
  Pallas kernels  38.6 us (98%)
  between operations  0.64 us (2%)
    pallas_call x1, Pallas kernels, local(): pl.pallas_call(functools.partial(kernel, seq_size, chosen), out_shape=(ja...  36.6 us
    pallas_call x1, Pallas kernels, local(): pl.pallas_call(settle_outputs, out_shape=(jax.ShapeDtypeStruct(attn.shape...  1.98 us

profile of v4, /device:TPU:0, one launch (start us, length us, event | category | flops | bytes accessed | tf_op | source)
XLA Modules:
  0.0 39.3 jit_solution(10614703686735917833)
XLA Ops:
  0.6 36.6 %shard_map.84 = (bf16[256,512]{1,0:T(8,128)(2,1)}, f32[256,512]{1,0:T(8,128)}, f32[128,256]{1,0:T(8,128)}) custom-call(s32[2,2,4]{2,1,0:T(2,128)} %bitcast.9, bf16[64,256]{1,0:T(8,128)(2,1)} %bitcast.7, bf16[64,256]{1,0:T(8,128)(2,1)} %bitcast.8, bf16[256,512]{1,0:T(8,128)(2,1)} %q_hbm.1, bf16[256,512]{1,0:T(8,128)(2,1)} %g_hbm.1), custom_call_target="tpu_custom_call" | custom-call | flops 2013265920 | bytes 2097152 | tf_op jit(solution)/shard_map/pallas_call | solution.py:344
  37.3 2.0 %shard_map.85 = (bf16[256,512]{1,0:T(8,128)(2,1)}, f32[256,512]{1,0:T(8,128)}, f32[64,256]{1,0:T(8,128)}, f32[64,256]{1,0:T(8,128)}) custom-call(bf16[256,512]{1,0:T(8,128)(2,1)} %get-tuple-element.11.attn, f32[256,512]{1,0:T(8,128)} %get-tuple-element.12.dq, f32[128,256]{1,0:T(8,128)} %get-tuple-element.13.grads), custom_call_target="tpu_custom_call" | custom-call | bytes 1835008 | tf_op jit(solution)/shard_map/pallas_call | solution.py:399

commit v5 on v4

v5 whole, which is shorter than its diff:
```python
import functools

import jax
import jax.numpy as jnp
from jax import lax
from jax.experimental import pallas as pl
from jax.experimental.pallas import tpu as pltpu
from jax.sharding import PartitionSpec as P

BLOCK = 512
NEGATIVE = -1e30
LOG2E = 1.4426950408889634
MESH = pl.DeviceIdType.MESH
F32 = jnp.float32
BF16 = jnp.bfloat16


def dot(a, b, contract):
    return lax.dot_general(a, b, ((contract[:1], contract[1:]), ((), ())), preferred_element_type=F32)


def places():
    seq = lax.axis_index("seq")
    head = lax.axis_index("head")
    b, c = seq // 2, seq % 2
    x, group = head % 2, head // 2
    return head, group, b, c, 1 - c, x, 1 - x, (2 * b + 1 - c, head), (seq, 2 * group + 1 - x)


def remote(src, dst, send, recv, dev):
    return pltpu.make_async_remote_copy(
        src_ref=src, dst_ref=dst, send_sem=send, recv_sem=recv, device_id=dev, device_id_type=MESH
    )


def greet(devices):
    barrier = pltpu.get_barrier_semaphore()
    for device in devices:
        pl.semaphore_signal(barrier, inc=1, device_id=device, device_id_type=MESH)
    pl.semaphore_wait(barrier, len(devices))


def gather(k_in, v_in, kv, zs, zr, xs, xr, cs, cr):
    half = k_in.shape[0]
    num_blocks = kv.shape[0]
    head, group, b, c, oc, x, ox, core_dev, x_dev = places()
    kv[b, c, x, :half] = k_in[...]
    kv[b, c, x, half:] = v_in[...]
    greet([core_dev, x_dev] + [(2 * lax.rem(b + d, num_blocks) + c, head) for d in range(1, num_blocks)])

    def z_gather(d):
        piece = kv.at[b - d, c, x]
        return remote(piece, piece, zs.at[d], zr.at[d + 1], (2 * (b + 1) + c, head))

    def z_arrival(d):
        piece = kv.at[b - d, c, x]
        return remote(piece, piece, zs.at[d], zr.at[d], (2 * (b - 1) + c, head))

    def x_gather(d, side):
        piece = kv.at[b - d, c, side]
        return remote(piece, piece, xs.at[d], xr.at[d], x_dev)

    def core_gather(d, which, row_half):
        piece = kv.at[b - d, row_half, x if which == 0 else ox]
        return remote(piece, piece, cs.at[d, which], cr.at[d, which], core_dev)

    x_gather(0, x).start()
    @pl.when(b + 1 < num_blocks)
    def _():
        z_gather(0).start()
    core_gather(0, 0, c).start()

    def forward_z(d):
        @pl.when(d <= b)
        def _():
            z_arrival(d).wait_recv()
            x_gather(d, x).start()
            if d + 1 < num_blocks:
                @pl.when(b + 1 < num_blocks)
                def _():
                    z_gather(d).start()
            core_gather(d, 0, c).start()

    def forward_x(d):
        @pl.when(d <= b)
        def _():
            x_gather(d, ox).wait_recv()
            core_gather(d, 1, c).start()

    def settle(d):
        @pl.when(d <= b)
        def _():
            core_gather(d, 0, oc).wait_recv()
            core_gather(d, 1, oc).wait_recv()

    forward_x(0)
    for d in range(1, num_blocks):
        forward_z(d)
        forward_x(d - 1) if d > 1 else None
    if num_blocks > 1:
        forward_x(num_blocks - 1)
    for d in range(num_blocks):
        settle(d)
    for d in range(num_blocks):
        @pl.when(d <= b)
        def _():
            x_gather(d, x).wait_send()
            core_gather(d, 0, c).wait_send()
            core_gather(d, 1, c).wait_send()
    for d in range(num_blocks - 1):
        @pl.when((d <= b) & (b + 1 < num_blocks))
        def _():
            z_gather(d).wait_send()


def compute(
    chosen, picks, kv, q_hbm, g_hbm, attn_hbm, dq_hbm, part,
    q4, g4, k_low, v_low, ev, dpv, p_low, ds_low, k_t, v_t, top, total, prod, attn_buf, dq_buf, in_sem, out_sem,
):
    dim, rows = kv.shape[3:]
    half = dim // 2
    heads = q4.shape[0]
    head, group, b, c = places()[:4]
    scaling = dim ** (-0.5)
    rate = scaling * LOG2E
    part_rows = rows // 2

    loads = []
    for h in range(heads):
        cols = pl.ds(h * dim, dim)
        loads.append(pltpu.make_async_copy(q_hbm.at[:, cols], q4.at[h], in_sem.at[0, h]))
        loads.append(pltpu.make_async_copy(g_hbm.at[:, cols], g4.at[h], in_sem.at[1, h]))
    for load in loads:
        load.start()

    def tiles(block):
        wide = [jnp.concatenate([kv[block, 0, side], kv[block, 1, side]], axis=1) for side in range(2)]
        keys = jnp.concatenate([wide[0][:half], wide[1][:half]], axis=0)
        values = jnp.concatenate([wide[0][half:], wide[1][half:]], axis=0)
        return keys, values

    def prepare(slot, block):
        key_tile, value_tile = tiles(block)
        for piece in range(4):
            side, chunk = piece % 2, piece // 2
            cut = slice(side * rows + chunk * part_rows, side * rows + (chunk + 1) * part_rows)
            at = pl.ds(pl.multiple_of(slot * BLOCK + piece * part_rows, part_rows), part_rows)
            k_t[:, at] = key_tile[:, cut]
            v_t[:, at] = value_tile[:, cut]
        k_low[slot] = key_tile.astype(F32).T.astype(BF16)
        v_low[slot] = value_tile.astype(F32).T.astype(BF16)

    def first_pass(slot, which, usable, causal):
        for h in which:
            s = dot(k_low[slot], q4[h], (1, 1))
            if causal:
                place = lax.broadcasted_iota(jnp.int32, (BLOCK, rows), 0)
                query = lax.broadcasted_iota(jnp.int32, (BLOCK, rows), 1) + c * rows
                s = jnp.where(place <= query, s, NEGATIVE)
            dp = dot(v_low[slot], g4[h], (1, 1))
            m = jnp.max(s, axis=0, keepdims=True)
            e = jnp.exp2((s - m) * rate)
            for piece in range(4):
                side, chunk = piece % 2, piece // 2
                cut = slice(side * rows + chunk * part_rows, side * rows + (chunk + 1) * part_rows)
                at = slice(side * part_rows, (side + 1) * part_rows)
                ev[2 * slot + chunk, h, at] = e[cut]
                dpv[2 * slot + chunk, h, at] = dp[cut]
            top[slot, h] = m if causal else jnp.where(usable, m, NEGATIVE)
            total[slot, h] = jnp.sum(e, axis=0, keepdims=True)
            prod[slot, h] = jnp.sum(e * dp, axis=0, keepdims=True)

    every = list(range(heads))
    prepare(0, b)
    for load in loads:
        load.wait()
    first_pass(0, every, None, True)

    @pl.loop(1, chosen)
    def _(slot):
        wanted = b - picks[group, slot - 1, b]
        prepare(slot, jnp.maximum(wanted, 0))
        first_pass(slot, every, wanted >= 0, False)

    for h in every:
        m = top[0, h]
        for slot in range(1, chosen):
            m = jnp.maximum(m, top[slot, h])
        weight = [jnp.exp2((top[slot, h] - m) * rate) for slot in range(chosen)]
        norm = sum(weight[slot] * total[slot, h] for slot in range(chosen))
        share = [w / norm for w in weight]
        for slot in range(chosen):
            top[slot, h] = share[slot]
        total[0, h] = sum(share[slot] * prod[slot, h] for slot in range(chosen))

    def second_pass(unit):
        slot = unit // 2
        at = pl.ds(pl.multiple_of(unit * 2 * part_rows, 2 * part_rows), 2 * part_rows)
        grad_k = grad_v = 0.0
        for h in every:
            cols = slice(h * rows, (h + 1) * rows)
            probs = ev[unit, h] * top[slot, h]
            low = probs.astype(BF16)
            ds = (probs * (dpv[unit, h] - total[0, h])).astype(BF16)
            p_low[at, cols] = low
            ds_low[at, cols] = ds
            grad_v += dot(low, g4[h], (1, 0))
            grad_k += dot(ds, q4[h], (1, 0))
        grad_k = grad_k * scaling
        lanes = lax.broadcasted_iota(jnp.int32, grad_k.shape, 1) < half
        left = jnp.where(lanes, grad_k, pltpu.roll(grad_v, half, 1)).astype(BF16)
        right = jnp.where(lanes, pltpu.roll(grad_k, half, 1), grad_v).astype(BF16)
        for side in range(2):
            cut = slice(side * part_rows, (side + 1) * part_rows)
            part[unit, side, 0] = left[cut]
            part[unit, side, 1] = right[cut]

    @pl.loop(0, 2 * chosen)
    def _(unit):
        second_pass(unit)

    attn_buf[...] = dot(v_t[...], p_low[...], (1, 0)).T.astype(BF16)
    dq_buf[...] = (dot(k_t[...], ds_low[...], (1, 0)) * scaling).T
    stores = []
    for h in range(heads):
        at, cols = pl.ds(h * rows, rows), pl.ds(h * dim, dim)
        stores.append(pltpu.make_async_copy(attn_buf.at[at], attn_hbm.at[:, cols], out_sem.at[0, h]))
        stores.append(pltpu.make_async_copy(dq_buf.at[at], dq_hbm.at[:, cols], out_sem.at[1, h]))
        stores[-2].start()
        stores[-1].start()

    for store in stores:
        store.wait()


def give_back(chosen, picks, part, grads_out, core_in, x_out, x_in, summed, z_out, z_in, cs2, cr2, xs2, xr2, zs2, zr2):
    num_blocks = z_in.shape[0]
    part_rows = part.shape[3]
    head, group, b, c, oc, x, ox, core_dev, x_dev = places()
    greet([core_dev, x_dev] + [(2 * lax.rem(b + d, num_blocks) + c, head) for d in range(1, num_blocks)])

    def core_return(unit):
        return remote(part.at[unit, oc], core_in.at[unit], cs2.at[unit], cr2.at[unit], core_dev)

    def x_return(unit):
        return remote(x_out.at[unit], x_in.at[unit], xs2.at[unit], xr2.at[unit], x_dev)

    def z_return(d, chunk):
        return remote(
            z_out.at[d, chunk], z_in.at[d, chunk], zs2.at[d, chunk], zr2.at[d, chunk], (2 * (b - d) + c, head)
        )

    def cross(unit):
        core_return(unit).wait_recv()
        x_out[unit] = (part[unit, c, ox].astype(F32) + core_in[unit, ox].astype(F32)).astype(BF16)
        x_return(unit).start()
        summed[unit] = part[unit, c, x].astype(F32) + core_in[unit, x].astype(F32)

    def land(unit):
        x_return(unit).wait_recv()
        summed[unit] = summed[unit] + x_in[unit].astype(F32)

    def send_back(chunk):
        for slot in range(1, chosen):
            land(2 * slot + chunk)
        for d in reversed(range(1, num_blocks)):
            @pl.when(d <= b)
            def _():
                z_out[d, chunk] = sum(
                    jnp.where(picks[group, slot - 1, b] == d, summed[2 * slot + chunk], 0.0)
                    for slot in range(1, chosen)
                ).astype(BF16)
                z_return(d, chunk).start()

    order = [2 * slot + chunk for chunk in range(2) for slot in range(1, chosen)] + [0, 1]
    for unit in order:
        core_return(unit).start()
    for step, unit in enumerate(order):
        cross(unit)
        if step == 2 * chosen - 3:
            send_back(0)
    send_back(1)
    for chunk in range(2):
        land(chunk)
        for d in range(1, num_blocks):
            @pl.when(b + d < num_blocks)
            def _():
                z_return(d, chunk).wait_recv()
                summed[chunk] = summed[chunk] + z_in[d, chunk].astype(F32)
        at = pl.ds(chunk * part_rows, part_rows)
        grads_out[:, at] = summed[chunk].T

    for d in range(1, num_blocks):
        @pl.when(d <= b)
        def _():
            z_return(d, 0).wait_send()
            z_return(d, 1).wait_send()
    for unit in range(2 * chosen):
        core_return(unit).wait_send()
        x_return(unit).wait_send()


def local(queries, key_states, value_states, block_picks, grad_output):
    rows, half = key_states.shape
    dim = 2 * half
    heads = queries.shape[1] // dim
    num_blocks = lax.axis_size("seq") * rows // BLOCK
    assert BLOCK == 2 * rows
    chosen = block_picks.shape[2] + 1
    keys = chosen * BLOCK
    units = 2 * chosen
    vmem = pl.BlockSpec(memory_space=pltpu.VMEM)
    smem = pl.BlockSpec(memory_space=pltpu.SMEM)
    anywhere = pl.BlockSpec(memory_space=pl.ANY)
    dma = pltpu.SemaphoreType.DMA
    picks = block_picks.transpose(1, 2, 0)
    kv = pl.pallas_call(
        gather,
        out_shape=jax.ShapeDtypeStruct((num_blocks, 2, 2, dim, rows), BF16),
        in_specs=[vmem, vmem],
        out_specs=vmem,
        scratch_shapes=[dma((num_blocks,))] * 4 + [dma((num_blocks, 2))] * 2,
        compiler_params=pltpu.CompilerParams(
            collective_id=0, has_side_effects=True, vmem_limit_bytes=24 * 1024 * 1024
        ),
    )(key_states.T, value_states.T)
    attn, dq, part = pl.pallas_call(
        functools.partial(compute, chosen),
        out_shape=(
            jax.ShapeDtypeStruct(queries.shape, BF16),
            jax.ShapeDtypeStruct(queries.shape, F32),
            jax.ShapeDtypeStruct((units, 2, 2, rows // 2, dim), BF16),
        ),
        in_specs=[smem, vmem, anywhere, anywhere],
        out_specs=(anywhere, anywhere, vmem),
        scratch_shapes=[
            pltpu.VMEM((heads, rows, dim), BF16),
            pltpu.VMEM((heads, rows, dim), BF16),
            pltpu.VMEM((chosen, BLOCK, dim), BF16),
            pltpu.VMEM((chosen, BLOCK, dim), BF16),
            pltpu.VMEM((units, heads, rows, rows), F32),
            pltpu.VMEM((units, heads, rows, rows), F32),
            pltpu.VMEM((keys, heads * rows), BF16),
            pltpu.VMEM((keys, heads * rows), BF16),
            pltpu.VMEM((dim, keys), BF16),
            pltpu.VMEM((dim, keys), BF16),
            pltpu.VMEM((chosen, heads, 1, rows), F32),
            pltpu.VMEM((chosen, heads, 1, rows), F32),
            pltpu.VMEM((chosen, heads, 1, rows), F32),
            pltpu.VMEM((heads * rows, dim), BF16),
            pltpu.VMEM((heads * rows, dim), F32),
            dma((2, heads)),
            dma((2, heads)),
        ],
        compiler_params=pltpu.CompilerParams(vmem_limit_bytes=48 * 1024 * 1024),
        cost_estimate=pl.CostEstimate(
            flops=10 * heads * rows * keys * dim, bytes_accessed=20 * queries.size, transcendentals=heads * rows * keys
        ),
    )(picks, kv, queries, grad_output)
    grads = pl.pallas_call(
        functools.partial(give_back, chosen),
        out_shape=jax.ShapeDtypeStruct((dim, rows), F32),
        in_specs=[smem, vmem],
        out_specs=vmem,
        scratch_shapes=[
            pltpu.VMEM((units, 2, rows // 2, dim), BF16),
            pltpu.VMEM((units, rows // 2, dim), BF16),
            pltpu.VMEM((units, rows // 2, dim), BF16),
            pltpu.VMEM((units, rows // 2, dim), F32),
            pltpu.VMEM((num_blocks, 2, rows // 2, dim), BF16),
            pltpu.VMEM((num_blocks, 2, rows // 2, dim), BF16),
        ]
        + [dma((units,))] * 4
        + [dma((num_blocks, 2))] * 2,
        compiler_params=pltpu.CompilerParams(
            collective_id=1, has_side_effects=True, vmem_limit_bytes=24 * 1024 * 1024
        ),
    )(picks, part)
    return attn, dq, grads[:half].T, grads[half:].T


def solution(mesh):
    return jax.shard_map(
        local,
        mesh=mesh,
        in_specs=(P("seq", "head"), P("seq", "head"), P("seq", "head"), P(), P("seq", "head")),
        out_specs=(P("seq", "head"), P("seq", "head"), P("seq", "head"), P("seq", "head")),
        check_vma=False,
    )
```

time: 39.5 us -> 46.3 us (1.17)
  Pallas kernels: 38.6 us -> 43.2 us
  local copies, waits for them, and re-layouts: 0 us -> 2.18 us
    pallas_call x2 -> x3, Pallas kernels: 38.6 us -> 43.2 us  [the longest x1 23.6 us: local(): pl.pallas_call(functools.partial(give_back, chosen), out_shape=jax.ShapeD...]
    unnamed x0 -> x10, local copies, waits for them, and re-layouts: none -> 1.52 us
    transpose x0 -> x1, local copies, waits for them, and re-layouts: none -> 0.66 us  [local(): return (attn, dq, grads[:half].T, grads[half:].T)]
where the time goes in v5:
time: 46.3 us; the launch traced here: 46.1 us
  Pallas kernels  43.2 us (93%)
  local copies, waits for them, and re-layouts  2.18 us (5%)
  between operations  0.69 us (1%)
    pallas_call x1, Pallas kernels, local(): pl.pallas_call(functools.partial(give_back, chosen), out_shape=jax.ShapeD...  23.6 us
    pallas_call x1, Pallas kernels, local(): pl.pallas_call(gather, out_shape=jax.ShapeDtypeStruct((num_blocks, 2, 2,...  10 us
    pallas_call x1, Pallas kernels, local(): pl.pallas_call(functools.partial(compute, chosen), out_shape=(jax.ShapeDt...  9.53 us
    unnamed x10, local copies, waits for them, and re-layouts  1.52 us

profile of v5, /device:TPU:0, one launch (start us, length us, event | category | flops | bytes accessed | tf_op | source)
XLA Modules:
  0.0 46.1 jit_solution(18220776238149084167)
XLA Ops:
  0.6 0.0 copy-start
  0.6 0.7 %copy-done = bf16[256,64]{0,1:T(8,128)(2,1)S(1)} copy-done((bf16[256,64]{0,1:T(8,128)(2,1)S(1)}, bf16[256,64]{0,1:T(8,128)(2,1)}, u32[]{:S(2)}) %copy-start) | copy-done | bytes 32792
  1.4 0.0 copy-start.1
  1.4 0.8 %copy-done.1 = bf16[256,64]{0,1:T(8,128)(2,1)S(1)} copy-done((bf16[256,64]{0,1:T(8,128)(2,1)S(1)}, bf16[256,64]{0,1:T(8,128)(2,1)}, u32[]{:S(2)}) %copy-start.1) | copy-done | bytes 32792
  2.1 0.0 copy-start.2
  2.2 0.0 copy-start.3
  2.2 0.0 copy-start.4
  2.2 10.0 %shard_map.84.kv = bf16[4,2,2,128,256]{4,3,2,1,0:T(8,128)(2,1)S(1)} custom-call(bf16[64,256]{1,0:T(8,128)(2,1)S(1)} %bitcast.7, bf16[64,256]{1,0:T(8,128)(2,1)S(1)} %bitcast.8), custom_call_target="tpu_custom_call" | custom-call | tf_op jit(solution)/shard_map/pallas_call | solution.py:317
  12.2 0.0 copy-done.2
  12.2 0.0 copy-done.3
  12.2 0.0 copy-done.4
  12.2 9.5 %shard_map.85 = (bf16[256,512]{1,0:T(8,128)(2,1)}, f32[256,512]{1,0:T(8,128)}, bf16[6,2,2,128,128]{4,3,2,1,0:T(8,128)(2,1)S(1)}) custom-call(s32[2,2,4]{2,1,0:T(2,128)S(1)} %bitcast.9, bf16[4,2,2,128,256]{4,3,2,1,0:T(8,128)(2,1)S(1)} %shard_map.84.kv, bf16[256,512]{1,0:T(8,128)(2,1)S(1)} %copy-done.3, bf16[256,512]{1,0:T(8,128)(2,1)S(1)} %copy-done.4), custom_call_target="tpu_custom_call" | custom-call | flops 2013265920 | bytes 2621440 | tf_op jit(solution)/shard_map/pallas_call | solution.py:327
  21.8 23.6 %shard_map.86 = f32[128,256]{1,0:T(8,128)S(1)} custom-call(s32[2,2,4]{2,1,0:T(2,128)S(1)} %bitcast.10, bf16[6,2,2,128,128]{4,3,2,1,0:T(8,128)(2,1)S(1)} %get-tuple-element.9.part), custom_call_target="tpu_custom_call" | custom-call | tf_op jit(solution)/shard_map/pallas_call | solution.py:360
  45.4 0.7 %slice_bitcast_fusion = (f32[256,64]{0,1:T(8,128)}, f32[256,64]{0,1:T(8,128)}) fusion(f32[128,256]{1,0:T(8,128)S(1)} %shard_map.86), kind=kLoop, calls=%fused_computation | loop fusion | bytes 262144 | tf_op jit(solution)/shard_map/transpose | solution.py:379
Async XLA Ops:
  0.6 0.8 %copy-start = (bf16[256,64]{0,1:T(8,128)(2,1)S(1)}, bf16[256,64]{0,1:T(8,128)(2,1)}, u32[]{:S(2)}) copy-start(bf16[256,64]{0,1:T(8,128)(2,1)} %param.6) | copy-start | bytes 98308
  1.4 0.8 %copy-start.1 = (bf16[256,64]{0,1:T(8,128)(2,1)S(1)}, bf16[256,64]{0,1:T(8,128)(2,1)}, u32[]{:S(2)}) copy-start(bf16[256,64]{0,1:T(8,128)(2,1)} %param.7) | copy-start | bytes 98308
  2.1 10.0 %copy-start.2 = (s32[4,2,2]{0,2,1:T(2,128)S(1)}, s32[4,2,2]{0,2,1:T(2,128)}, u32[]{:S(2)}) copy-start(s32[4,2,2]{0,2,1:T(2,128)} %param.8) | copy-start | bytes 196
  2.2 10.1 %copy-start.3 = (bf16[256,512]{1,0:T(8,128)(2,1)S(1)}, bf16[256,512]{1,0:T(8,128)(2,1)}, u32[]{:S(2)}) copy-start(bf16[256,512]{1,0:T(8,128)(2,1)} %q_hbm.1) | copy-start | bytes 786436
  2.2 10.1 %copy-start.4 = (bf16[256,512]{1,0:T(8,128)(2,1)S(1)}, bf16[256,512]{1,0:T(8,128)(2,1)}, u32[]{:S(2)}) copy-start(bf16[256,512]{1,0:T(8,128)(2,1)} %g_hbm.1) | copy-start | bytes 786436

commit v6 on v4

--- a/solution.py
+++ b/solution.py
@@ -23,7 +23,7 @@
     seq_size, chosen, picks, k_in, v_in, q_hbm, g_hbm, attn_hbm, dq_hbm, grads_out,
     kv, q4, g4, k_low, v_low, ev, dpv, p_low, ds_low, k_t, v_t, top, total, prod, attn_buf, dq_buf,
     part, core_in, x_out, x_in, summed, z_out, z_in,
-    in_sem, out_sem, zs, zr, xs, xr, cs, cr, cs2, cr2, xs2, xr2, zs2, zr2,
+    in_sem, out_sem, own_sem, zs, zr, xs, xr, cs, cr, cs2, cr2, xs2, xr2, zs2, zr2,
 ):
     half, rows = k_in.shape
     dim = 2 * half
@@ -50,7 +50,11 @@
         cols = pl.ds(h * dim, dim)
         loads.append(pltpu.make_async_copy(q_hbm.at[:, cols], q4.at[h], in_sem.at[0, h]))
         loads.append(pltpu.make_async_copy(g_hbm.at[:, cols], g4.at[h], in_sem.at[1, h]))
-    for load in loads:
+    own_loads = [
+        pltpu.make_async_copy(ref, kv.at[b, c, x, pl.ds(kind * half, half)], own_sem.at[kind])
+        for kind, ref in enumerate((k_in, v_in))
+    ]
+    for load in own_loads + loads:
         load.start()
 
     barrier = pltpu.get_barrier_semaphore()
@@ -59,54 +63,57 @@
     for d in range(1, num_blocks):
         other = lax.rem(b + d, num_blocks)
         pl.semaphore_signal(barrier, inc=1, device_id=(2 * other + c, head), device_id_type=MESH)
-    kv[b, c, x, :half] = k_in[...]
-    kv[b, c, x, half:] = v_in[...]
+    for load in own_loads:
+        load.wait()
     pl.semaphore_wait(barrier, num_blocks + 1)
 
-    def z_gather(d):
-        piece = kv.at[b - d, c, x]
-        return remote(piece, piece, zs.at[d], zr.at[d + 1], (2 * (b + 1) + c, head))
-
-    def z_arrival(d):
-        piece = kv.at[b - d, c, x]
-        return remote(piece, piece, zs.at[d], zr.at[d], (2 * (b - 1) + c, head))
-
-    def x_gather(d, side):
-        piece = kv.at[b - d, c, side]
-        return remote(piece, piece, xs.at[d], xr.at[d], x_dev)
-
-    def core_gather(d, which, row_half):
-        piece = kv.at[b - d, row_half, x if which == 0 else ox]
-        return remote(piece, piece, cs.at[d, which], cr.at[d, which], core_dev)
-
-    x_gather(0, x).start()
-    @pl.when(b + 1 < num_blocks)
-    def _():
-        z_gather(0).start()
-    core_gather(0, 0, c).start()
-
-    def forward_z(d):
+    def piece(d, row_half, side, part_of):
+        return kv.at[b - d, row_half, side, pl.ds(part_of * half, half)]
+
+    def z_gather(d, kind):
+        mine = piece(0, c, x, kind)
+        return remote(mine, mine, zs.at[d, kind], zr.at[d, kind], (2 * (b + d) + c, head))
+
+    def z_arrival(d, kind):
+        there = piece(d, c, x, kind)
+        return remote(there, there, zs.at[d, kind], zr.at[d, kind], (2 * (b - d) + c, head))
+
+    def x_gather(d, side, kind):
+        there = piece(d, c, side, kind)
+        return remote(there, there, xs.at[d, kind], xr.at[d, kind], x_dev)
+
+    def core_gather(d, which, row_half, kind):
+        there = piece(d, row_half, x if which == 0 else ox, kind)
+        return remote(there, there, cs.at[d, which, kind], cr.at[d, which, kind], core_dev)
+
+    for kind in range(2):
+        x_gather(0, x, kind).start()
+        for d in reversed(range(1, num_blocks)):
+            @pl.when(b + d < num_blocks)
+            def _():
+                z_gather(d, kind).start()
+    for kind in range(2):
+        core_gather(0, 0, c, kind).start()
+
+    def forward_z(d, kind):
         @pl.when(d <= b)
         def _():
-            z_arrival(d).wait_recv()
-            x_gather(d, x).start()
-            if d + 1 < num_blocks:
-                @pl.when(b + 1 < num_blocks)
-                def _():
-                    z_gather(d).start()
-            core_gather(d, 0, c).start()
-
-    def forward_x(d):
+            z_arrival(d, kind).wait_recv()
+            x_gather(d, x, kind).start()
+            core_gather(d, 0, c, kind).start()
+
+    def forward_x(d, kind):
         @pl.when(d <= b)
         def _():
-            x_gather(d, ox).wait_recv()
-            core_gather(d, 1, c).start()
+            x_gather(d, ox, kind).wait_recv()
+            core_gather(d, 1, c, kind).start()
 
     def settle(d):
         @pl.when(d <= b)
         def _():
-            core_gather(d, 0, oc).wait_recv()
-            core_gather(d, 1, oc).wait_recv()
+            for kind in range(2):
+                core_gather(d, 0, oc, kind).wait_recv()
+                core_gather(d, 1, oc, kind).wait_recv()
 
     def tiles(block):
         wide = [jnp.concatenate([kv[block, 0, side], kv[block, 1, side]], axis=1) for side in range(2)]
@@ -146,30 +153,24 @@
             prod[slot, h] = jnp.sum(e * dp, axis=0, keepdims=True)
 
     every = list(range(heads))
-    forward_x(0)
-    for d in range(1, min(3, num_blocks)):
-        forward_z(d)
-        if d == 1:
-            forward_x(d)
+    earlier = range(1, num_blocks)
+    forward_x(0, 0)
+    forward_x(0, 1)
+    for kind in range(2):
+        for d in earlier:
+            forward_z(d, kind)
+    for d in earlier:
+        forward_x(d, 0)
     for load in loads:
         load.wait()
     settle(0)
     prepare(0, b)
-    first_pass(0, every[: heads // 2], None, True)
-    if num_blocks > 2:
-        forward_x(2)
-    if num_blocks > 3:
-        forward_z(3)
-    first_pass(0, every[heads // 2 :], None, True)
-    if num_blocks > 3:
-        forward_x(3)
-    for d in range(4, num_blocks):
-        forward_z(d)
-        forward_x(d)
-    for d in range(1, num_blocks):
+    first_pass(0, every, None, True)
+    for d in earlier:
+        forward_x(d, 1)
+    for d in earlier:
         settle(d)
 
-    offsets = [None] + [picks[group, j, b] for j in range(chosen - 1)]
     @pl.loop(1, chosen)
     def _(slot):
         wanted = b - picks[group, slot - 1, b]
@@ -290,13 +291,15 @@
     for d in range(num_blocks):
         @pl.when(d <= b)
         def _():
-            x_gather(d, x).wait_send()
-            core_gather(d, 0, c).wait_send()
-            core_gather(d, 1, c).wait_send()
-    for d in range(num_blocks - 1):
-        @pl.when((d <= b) & (b + 1 < num_blocks))
-        def _():
-            z_gather(d).wait_send()
+            for kind in range(2):
+                x_gather(d, x, kind).wait_send()
+                core_gather(d, 0, c, kind).wait_send()
+                core_gather(d, 1, c, kind).wait_send()
+    for d in range(1, num_blocks):
+        @pl.when(b + d < num_blocks)
+        def _():
+            z_gather(d, 0).wait_send()
+            z_gather(d, 1).wait_send()
     for d in range(1, num_blocks):
         @pl.when(d <= b)
         def _():
@@ -348,7 +351,7 @@
             jax.ShapeDtypeStruct(queries.shape, F32),
             jax.ShapeDtypeStruct((dim, rows), F32),
         ),
-        in_specs=[pl.BlockSpec(memory_space=pltpu.SMEM), vmem, vmem, anywhere, anywhere],
+        in_specs=[pl.BlockSpec(memory_space=pltpu.SMEM)] + [anywhere] * 4,
         out_specs=(anywhere, anywhere, vmem),
         scratch_shapes=[
             pltpu.VMEM((num_blocks, 2, 2, dim, rows), BF16),
@@ -376,12 +379,13 @@
             pltpu.VMEM((num_blocks, 2, rows // 2, dim), BF16),
             dma((2, heads)),
             dma((2, heads)),
-            dma((num_blocks,)),
-            dma((num_blocks,)),
-            dma((num_blocks,)),
-            dma((num_blocks,)),
-            dma((num_blocks, 2)),
-            dma((num_blocks, 2)),
+            dma((2,)),
+            dma((num_blocks, 2)),
+            dma((num_blocks, 2)),
+            dma((num_blocks, 2)),
+            dma((num_blocks, 2)),
+            dma((num_blocks, 2, 2)),
+            dma((num_blocks, 2, 2)),
             dma((2 * chosen,)),
             dma((2 * chosen,)),
             dma((2 * chosen,)),

time: 39.5 us -> 37.3 us (0.944)
  Pallas kernels: 38.6 us -> 36.4 us
    pallas_call x1, Pallas kernels: 36.6 us -> 34.5 us  [local(): pl.pallas_call(functools.partial(kernel, seq_size, chosen), out_shape=(ja...]
where the time goes in v6:
time: 37.3 us; the launch traced here: 37.1 us
  Pallas kernels  36.4 us (98%)
  between operations  0.64 us (2%)
    pallas_call x1, Pallas kernels, local(): pl.pallas_call(functools.partial(kernel, seq_size, chosen), out_shape=(ja...  34.5 us
    pallas_call x1, Pallas kernels, local(): pl.pallas_call(settle_outputs, out_shape=(jax.ShapeDtypeStruct(attn.shape...  1.98 us

profile of v6, /device:TPU:0, one launch (start us, length us, event | category | flops | bytes accessed | tf_op | source)
XLA Modules:
  0.0 37.1 jit_solution(7582698756276538543)
XLA Ops:
  0.6 34.5 %shard_map.84 = (bf16[256,512]{1,0:T(8,128)(2,1)}, f32[256,512]{1,0:T(8,128)}, f32[128,256]{1,0:T(8,128)}) custom-call(s32[2,2,4]{2,1,0:T(2,128)} %bitcast.9, bf16[64,256]{1,0:T(8,128)(2,1)} %bitcast.7, bf16[64,256]{1,0:T(8,128)(2,1)} %bitcast.8, bf16[256,512]{1,0:T(8,128)(2,1)} %q_hbm.1, bf16[256,512]{1,0:T(8,128)(2,1)} %g_hbm.1), custom_call_target="tpu_custom_call" | custom-call | flops 2013265920 | bytes 2097152 | tf_op jit(solution)/shard_map/pallas_call | solution.py:347
  35.1 2.0 %shard_map.85 = (bf16[256,512]{1,0:T(8,128)(2,1)}, f32[256,512]{1,0:T(8,128)}, f32[64,256]{1,0:T(8,128)}, f32[64,256]{1,0:T(8,128)}) custom-call(bf16[256,512]{1,0:T(8,128)(2,1)} %get-tuple-element.11.attn, f32[256,512]{1,0:T(8,128)} %get-tuple-element.12.dq, f32[128,256]{1,0:T(8,128)} %get-tuple-element.13.grads), custom_call_target="tpu_custom_call" | custom-call | bytes 1835008 | tf_op jit(solution)/shard_map/pallas_call | solution.py:403

commit v7 on v6

--- a/solution.py
+++ b/solution.py
@@ -255,14 +255,15 @@
     def _(step):
         second_pass(unit_of(step))
 
-        @pl.when(step > 0)
-        def _():
-            cross(unit_of(step - 1))
-
-        @pl.when(step == 2 * others - 1)
+        @pl.when(step > 1)
+        def _():
+            cross(unit_of(step - 2))
+
+        @pl.when(step == 2 * others)
         def _():
             send_back(0)
 
+    cross(0)
     send_back(1)
     cross(1)
 

time: 37.3 us -> 37.6 us (level)
  Pallas kernels: 36.4 us -> 36.8 us
where the time goes in v7:
time: 37.6 us; the launch traced here: 37.4 us
  Pallas kernels  36.8 us (98%)
  between operations  0.64 us (2%)
    pallas_call x1, Pallas kernels, local(): pl.pallas_call(functools.partial(kernel, seq_size, chosen), out_shape=(ja...  34.8 us
    pallas_call x1, Pallas kernels, local(): pl.pallas_call(settle_outputs, out_shape=(jax.ShapeDtypeStruct(attn.shape...  1.98 us

profile of v7, /device:TPU:0, one launch (start us, length us, event | category | flops | bytes accessed | tf_op | source)
XLA Modules:
  0.0 37.4 jit_solution(6513129828821520670)
XLA Ops:
  0.6 34.8 %shard_map.84 = (bf16[256,512]{1,0:T(8,128)(2,1)}, f32[256,512]{1,0:T(8,128)}, f32[128,256]{1,0:T(8,128)}) custom-call(s32[2,2,4]{2,1,0:T(2,128)} %bitcast.9, bf16[64,256]{1,0:T(8,128)(2,1)} %bitcast.7, bf16[64,256]{1,0:T(8,128)(2,1)} %bitcast.8, bf16[256,512]{1,0:T(8,128)(2,1)} %q_hbm.1, bf16[256,512]{1,0:T(8,128)(2,1)} %g_hbm.1), custom_call_target="tpu_custom_call" | custom-call | flops 2013265920 | bytes 2097152 | tf_op jit(solution)/shard_map/pallas_call | solution.py:348
  35.4 2.0 %shard_map.85 = (bf16[256,512]{1,0:T(8,128)(2,1)}, f32[256,512]{1,0:T(8,128)}, f32[64,256]{1,0:T(8,128)}, f32[64,256]{1,0:T(8,128)}) custom-call(bf16[256,512]{1,0:T(8,128)(2,1)} %get-tuple-element.11.attn, f32[256,512]{1,0:T(8,128)} %get-tuple-element.12.dq, f32[128,256]{1,0:T(8,128)} %get-tuple-element.13.grads), custom_call_target="tpu_custom_call" | custom-call | bytes 1835008 | tf_op jit(solution)/shard_map/pallas_call | solution.py:404
